TPU v7x, 1024 devices: a whole 8x8x8 slice. The times are simulated.
1024 devices in a mesh: node: 16 (over y, core), local: 64 (over z, x).
Axes of the slice: x: 8, y: 8, z: 8, core: 2. Of those that a mesh axis runs over, the one named last changes fastest.
Arguments:
- out_grad: bfloat16 [8192, 7168], P(('node', 'local')), may hold values from -6 to 6
- expert_ids: int32 [8192, 8], P(('node', 'local')), may hold values from 0 to 127, as said below
- route_weights: bfloat16 [8192, 8], P(('node', 'local')), may hold values from 0.099609375 to 0.59765625
- down_weight: bfloat16 [1024, 1024, 896], P(('node', 'local')), may hold values from -0.0625 to 0.0625
- gate_pre: bfloat16 [1024, 1024, 128], P(('node', 'local')), may hold values from -6 to 6
- up_pre: bfloat16 [1024, 1024, 128], P(('node', 'local')), may hold values from -6 to 6
Outputs:
- grad_pre: bfloat16 [1024, 2, 1024, 128], P(('node', 'local'))
- grad_weights: float32 [8192, 8], P(('node', 'local'))
Inputs may be any that keep to these rules, and one draw needn't show every extreme that they name: `expert_ids`: each token names 8 different experts, two in each of four different groups (expert e belongs to group e // 8). The 8 tokens of one device reach every group exactly 2 times. Of the 32 tokens on the devices of one local index that reach one group, at most 16 name any one expert of that group, and for every group and local index some expert is named by exactly 16 of them.
All inputs are finite; a program needn't handle non-finite values.
Results may differ from a plain program's by a relative error of at most 0.013.
Values may be sent and summed in bfloat16 or wider, within the bound.
No kernel may reach another device: no remote copies, remote signals or barrier semaphores. Data moves between devices by JAX's collectives and lax.ppermute only.
A program may use at most 32 MiB of HBM per device.

v0:
```python
import jax
import jax.numpy as jnp
from jax import lax
from jax.sharding import PartitionSpec as P

EPG = 8


def partner(x, axis, apart):
    return lax.ppermute(x, axis, [(i, i ^ 1 << apart) for i in range(lax.axis_size(axis))])


def body(out_grad, expert_ids, route_weights, down_weight, gate_pre, up_pre):
    n_node = lax.axis_size("node")
    n_local = lax.axis_size("local")
    tok_dev, model_width = out_grad.shape
    top_count = expert_ids.shape[1]
    shards = n_local // EPG
    piece_width = model_width // shards
    hidden_all = down_weight.shape[1]
    block_width = hidden_all // shards
    cap_group = 4 * tok_dev // n_node
    rows_relay = n_node * cap_group
    cap_expert = 2 * tok_dev
    slot_count = n_local * cap_expert
    group_iota = jnp.arange(n_node, dtype=jnp.int32)
    reaches = jnp.any((expert_ids // EPG)[:, :, None] == group_iota, axis=1).astype(jnp.int32)
    order_in = jnp.cumsum(reaches, axis=0) - reaches
    chosen = (reaches.T[:, None, :] == 1) & (
        order_in.T[:, None, :] == jnp.arange(cap_group, dtype=jnp.int32)[None, :, None]
    )
    send_rows = jnp.einsum(
        "gkt,td->gkd", chosen.astype(jnp.bfloat16), out_grad, preferred_element_type=jnp.float32
    ).astype(jnp.bfloat16)
    filled = jnp.sum(chosen.astype(jnp.int32), axis=2)
    send_ids = (
        jnp.sum(jnp.where(chosen[..., None], expert_ids[None, None], 0), axis=2)
        + filled[..., None]
        - 1
    )
    send_weights = jnp.sum(
        jnp.where(chosen[..., None], route_weights.astype(jnp.float32)[None, None], 0.0), axis=2
    ).astype(jnp.bfloat16)
    got_rows, got_ids, got_weights = (
        lax.all_to_all(send_rows, "node", split_axis=0, concat_axis=0, tiled=True),
        lax.all_to_all(send_ids, "node", split_axis=0, concat_axis=0, tiled=True),
        lax.all_to_all(send_weights, "node", split_axis=0, concat_axis=0, tiled=True),
    )
    relay_rows = got_rows.reshape(rows_relay, shards, piece_width)
    relay_ids = got_ids.reshape(rows_relay, top_count)
    relay_weights = got_weights.reshape(rows_relay, top_count).astype(jnp.float32)
    my_group = lax.axis_index("node")
    member = (relay_ids - my_group * EPG)[:, :, None] == jnp.arange(EPG, dtype=jnp.int32)
    named_by = jnp.any(member, axis=1).astype(jnp.int32)
    slot_of = jnp.cumsum(named_by, axis=0) - named_by
    row_code = (
        jnp.arange(rows_relay, dtype=jnp.int32)[:, None] * top_count
        + jnp.arange(top_count, dtype=jnp.int32)[None, :]
    )
    code_each = jnp.sum(jnp.where(member, row_code[:, :, None], 0), axis=1)
    weight_each = jnp.sum(jnp.where(member, relay_weights[:, :, None], 0.0), axis=1)
    assign = (named_by.T[:, None, :] == 1) & (
        slot_of.T[:, None, :] == jnp.arange(cap_expert, dtype=jnp.int32)[None, :, None]
    )
    spread_rows = (
        jnp.einsum(
            "ecr,rsd->escd",
            assign.astype(jnp.bfloat16),
            relay_rows,
            preferred_element_type=jnp.float32,
        )
        .astype(jnp.bfloat16)
        .reshape(n_local, cap_expert, piece_width)
    )
    is_used = jnp.any(assign, axis=2)
    slot_weight = jnp.sum(jnp.where(assign, weight_each.T[:, None, :], 0.0), axis=2)
    slot_code = jnp.where(
        is_used, jnp.sum(jnp.where(assign, code_each.T[:, None, :], 0), axis=2), -1
    )
    wide_weight = (
        jnp.broadcast_to(slot_weight[:, None], (EPG, shards, cap_expert))
        .reshape(n_local, cap_expert)
        .astype(jnp.bfloat16)
    )
    wide_code = jnp.broadcast_to(slot_code[:, None], (EPG, shards, cap_expert)).reshape(
        n_local, cap_expert
    )
    got_x, got_w, got_code = (
        lax.all_to_all(spread_rows, "local", split_axis=0, concat_axis=0, tiled=True),
        lax.all_to_all(wide_weight, "local", split_axis=0, concat_axis=0, tiled=True),
        lax.all_to_all(wide_code, "local", split_axis=0, concat_axis=0, tiled=True),
    )
    inputs = got_x.reshape(slot_count, piece_width)
    partial_value = lax.dot_general(
        inputs, down_weight[0], (((1,), (1,)), ((), ())), preferred_element_type=jnp.float32
    )
    partial_value = lax.optimization_barrier(partial_value.astype(jnp.bfloat16)).astype(jnp.float32)
    bit_count = shards.bit_length() - 1
    blocks = partial_value.reshape((slot_count,) + (2,) * bit_count + (block_width,))
    my_index = lax.axis_index("local")
    bit_order = list(range(bit_count - 1, -1, -1))
    for bit_index in bit_order:
        bit_dim = bit_count - bit_index
        my_bit = my_index >> bit_index & 1
        kept_half = lax.dynamic_index_in_dim(blocks, my_bit, bit_dim, keepdims=True)
        their_half = lax.dynamic_index_in_dim(blocks, 1 - my_bit, bit_dim, keepdims=True).astype(
            jnp.bfloat16
        )
        blocks = kept_half + partner(their_half, "local", bit_index).astype(jnp.float32)
    grad_hidden = blocks.reshape(slot_count, block_width)
    pre_gate = gate_pre[0].astype(jnp.float32)
    pre_up = up_pre[0].astype(jnp.float32)
    gating = jax.nn.sigmoid(pre_gate)
    silu_value = pre_gate * gating
    hidden_act = silu_value * pre_up
    scaled = got_w.reshape(slot_count, 1).astype(jnp.float32) * grad_hidden
    d_gate = scaled * pre_up * gating * (1.0 + pre_gate * (1.0 - gating))
    d_up = scaled * silu_value
    grad_pre = jnp.stack([d_gate, d_up], axis=0).astype(jnp.bfloat16)[None]
    partial_dot = jnp.sum(hidden_act * grad_hidden, axis=1).reshape(n_local, cap_expert)
    columns = jnp.arange(rows_relay * top_count, dtype=jnp.int32)
    returned = jnp.sum(
        jnp.where(got_code[:, :, None] == columns, partial_dot[:, :, None], 0.0), axis=1
    )
    returned = returned.reshape(n_local, n_node, cap_group, top_count)
    at_relay = jnp.sum(
        lax.all_to_all(
            returned.astype(jnp.bfloat16), "local", split_axis=0, concat_axis=0, tiled=True
        ).astype(returned.dtype),
        axis=0,
    )
    summed = lax.all_to_all(at_relay, "node", split_axis=0, concat_axis=0, tiled=True)
    grad_weights = jnp.sum(jnp.where(chosen[..., None], summed[:, :, None, :], 0.0), axis=(0, 1))
    return (grad_pre, grad_weights)


def solution(mesh):
    return jax.shard_map(
        body,
        mesh=mesh,
        in_specs=(
            P(("node", "local"), None),
            P(("node", "local"), None),
            P(("node", "local"), None),
            P(("node", "local"), None, None),
            P(("node", "local"), None, None),
            P(("node", "local"), None, None),
        ),
        out_specs=(P(("node", "local"), None, None, None), P(("node", "local"), None)),
        check_vma=False,
    )
```

profile of v0, /device:TPU:1, one launch (start us, length us, event | category | flops | bytes accessed | tf_op | source)
XLA Modules:
  0.0 288.0 jit_solution(5894376961461841489)
XLA Ops:
  3.1 17.4 %all-to-all-start = ((s32[16,2,8]{2,1,0:T(2,128)}), s32[16,2,8]{2,1,0:T(2,128)S(1)}, u32[]{:S(2)}, u32[]{:S(2)}) async-start(s32[16,2,8]{2,1,0:T(2,128)} %copy.107), calls=%async_computation | async-start | bytes 32768 | tf_op jit(solution)/shard_map/all_to_all | solution.py:46
  23.0 5.0 %all-to-all-done = s32[16,2,8]{2,1,0:T(2,128)S(1)} async-done(((s32[16,2,8]{2,1,0:T(2,128)}), s32[16,2,8]{2,1,0:T(2,128)S(1)}, u32[]{:S(2)}, u32[]{:S(2)}) %all-to-all-start) | async-done | bytes 1056 | tf_op jit(solution)/shard_map/all_to_all | solution.py:46
  27.9 3.7 %all-to-all-start.3 = ((bf16[16,2,7168]{2,1,0:T(2,128)(2,1)}), bf16[16,2,7168]{2,1,0:T(2,128)(2,1)S(1)}, u32[]{:S(2)}, u32[]{:S(2)}) async-start(bf16[16,2,7168]{2,1,0:T(2,128)(2,1)} %copy.115), calls=%async_computation.3 | async-start | bytes 917504 | tf_op jit(solution)/shard_map/all_to_all | solution.py:45
  32.1 15.6 %all-to-all-done.3 = bf16[16,2,7168]{2,1,0:T(2,128)(2,1)S(1)} async-done(((bf16[16,2,7168]{2,1,0:T(2,128)(2,1)}), bf16[16,2,7168]{2,1,0:T(2,128)(2,1)S(1)}, u32[]{:S(2)}, u32[]{:S(2)}) %all-to-all-start.3) | async-done | bytes 458784 | tf_op jit(solution)/shard_map/all_to_all | solution.py:45
  48.6 1.4 copy.117
  50.0 14.1 %all-to-all-start.4 = ((bf16[64,16,896]{2,1,0:T(8,128)(2,1)}), bf16[64,16,896]{2,1,0:T(8,128)(2,1)}, u32[]{:S(2)}, u32[]{:S(2)}) async-start(bf16[64,16,896]{2,1,0:T(8,128)(2,1)} %bitcast.79), calls=%async_computation.4 | async-start | bytes 3670016 | tf_op jit(solution)/shard_map/all_to_all | solution.py:89
  64.1 47.5 %all-to-all-done.4 = bf16[64,16,896]{2,1,0:T(8,128)(2,1)} async-done(((bf16[64,16,896]{2,1,0:T(8,128)(2,1)}), bf16[64,16,896]{2,1,0:T(8,128)(2,1)}, u32[]{:S(2)}, u32[]{:S(2)}) %all-to-all-start.4) | async-done | bytes 1835040 | tf_op jit(solution)/shard_map/all_to_all | solution.py:89
  111.6 5.2 %convolution_convert_fusion.1 = bf16[1024,1024]{1,0:T(8,128)(2,1)} fusion(bf16[1024,896]{1,0:T(8,128)(2,1)} %bitcast.13, bf16[1,1024,896]{2,1,0:T(8,128)(2,1)S(1)} %copy-done), kind=kOutput, calls=%fused_computation.3 | convolution fusion | flops 1880096768 | bytes 5767168 | tf_op jit(solution)/shard_map/dot_general | solution.py:94
  116.8 6.6 %reshape.205 = f32[1024,2,2,2,128]{4,3,2,1,0:T(2,128)} reshape(bf16[1024,1024]{1,0:T(8,128)(2,1)} %convolution_convert_fusion.1) | data formatting | bytes 6291456 | tf_op jit(solution)/shard_map/reshape | solution.py:99
  123.4 2.3 constant_dynamic-slice_fusion
  126.9 6.4 %collective-permute-start = (bf16[1024,1,2,2,128]{4,0,3,2,1:T(8,128)(2,1)}, bf16[1024,1,2,2,128]{4,0,3,2,1:T(8,128)(2,1)S(1)}, u32[]{:S(2)}, u32[]{:S(2)}) collective-permute-start(bf16[1024,1,2,2,128]{4,0,3,2,1:T(8,128)(2,1)} %copy.133), channel_id=1, source_target_pairs={{0,4},{1,5},{2,6},{3,7},{4,0},{5,1},{6,2},{7,3},{8,12},{9,13},{10,... | collective-permute-start | bytes 3145736 | tf_op jit(solution)/shard_map/ppermute | solution.py:10
  133.3 2.3 constant_dynamic-slice_fusion.1
  135.7 32.6 %collective-permute-done = bf16[1024,1,2,2,128]{4,0,3,2,1:T(8,128)(2,1)S(1)} collective-permute-done((bf16[1024,1,2,2,128]{4,0,3,2,1:T(8,128)(2,1)}, bf16[1024,1,2,2,128]{4,0,3,2,1:T(8,128)(2,1)S(1)}, u32[]{:S(2)}, u32[]{:S(2)}) %collective-permute-start) | collective-permute-done | bytes 1048608 | tf_op jit(solution)/shard_map/ppermute | solution.py:10
  168.5 14.9 %collective-permute-start.1 = (bf16[1024,1,1,2,128]{4,0,3,2,1:T(8,128)(2,1)S(1)}, bf16[1024,1,1,2,128]{4,0,3,2,1:T(8,128)(2,1)S(1)}, u32[]{:S(2)}, u32[]{:S(2)}) collective-permute-start(bf16[1024,1,1,2,128]{4,0,3,2,1:T(8,128)(2,1)S(1)} %dynamic-slice_convert_fusion), channel_id=1, source_target_pairs={{0,2},{1,3},{2,0},{3,1},{4,6},{5,7},{6,4},{7,5},{8,10},{9,11},{10,... | collective-permute-start | bytes 1572872 | tf_op jit(solution)/shard_map/ppermute | solution.py:10
  183.7 22.6 %collective-permute-done.1 = bf16[1024,1,1,2,128]{4,0,3,2,1:T(8,128)(2,1)S(1)} collective-permute-done((bf16[1024,1,1,2,128]{4,0,3,2,1:T(8,128)(2,1)S(1)}, bf16[1024,1,1,2,128]{4,0,3,2,1:T(8,128)(2,1)S(1)}, u32[]{:S(2)}, u32[]{:S(2)}) %collective-permute-start.1) | collective-permute-done | bytes 524320 | tf_op jit(solution)/shard_map/ppermute | solution.py:10
  207.1 3.1 %collective-permute-start.2 = (bf16[1024,1,1,1,128]{4,0,3,2,1:T(8,128)(2,1)}, bf16[1024,1,1,1,128]{4,0,3,2,1:T(8,128)(2,1)}, u32[]{:S(2)}, u32[]{:S(2)}) collective-permute-start(bf16[1024,1,1,1,128]{4,0,3,2,1:T(8,128)(2,1)} %dynamic-slice_convert_fusion.1), channel_id=1, source_target_pairs={{0,1},{1,0},{2,3},{3,2},{4,5},{5,4},{6,7},{7,6},{8,9},{9,8},{10,11... | collective-permute-start | bytes 786440 | tf_op jit(solution)/shard_map/ppermute | solution.py:10
  211.1 7.2 %all-to-all-start.5 = ((s32[64,1,16]{2,1,0:T(1,128)}), s32[64,1,16]{2,1,0:T(1,128)S(1)}, u32[]{:S(2)}, u32[]{:S(2)}) async-start(s32[64,1,16]{2,1,0:T(1,128)} %bitcast.19), calls=%async_computation.5 | async-start | bytes 65536 | tf_op jit(solution)/shard_map/all_to_all | solution.py:91
  219.6 9.5 %all-to-all-done.5 = s32[64,1,16]{2,1,0:T(1,128)S(1)} async-done(((s32[64,1,16]{2,1,0:T(1,128)}), s32[64,1,16]{2,1,0:T(1,128)S(1)}, u32[]{:S(2)}, u32[]{:S(2)}) %all-to-all-start.5) | async-done | bytes 4128 | tf_op jit(solution)/shard_map/all_to_all | solution.py:91
  230.1 14.6 %all_to_all.45 = bf16[64,2,128]{2,1,0:T(2,128)(2,1)S(1)} all-to-all(bf16[64,2,128]{2,1,0:T(2,128)(2,1)S(1)} %reshape.218), channel_id=1, replica_groups=mesh['node'=16,'local'=64] {'local'}, dimensions={0} | all-to-all | bytes 65536 | tf_op jit(solution)/shard_map/all_to_all | solution.py:127
  245.7 6.9 %all-to-all-start.7 = ((f32[16,2,8]{2,1,0:T(2,128)}), f32[16,2,8]{2,1,0:T(2,128)S(1)}, u32[]{:S(2)}, u32[]{:S(2)}) async-start(f32[16,2,8]{2,1,0:T(2,128)} %copy.122), calls=%async_computation.7 | async-start | bytes 32768 | tf_op jit(solution)/shard_map/all_to_all | solution.py:132
  252.6 7.4 %all-to-all-done.7 = f32[16,2,8]{2,1,0:T(2,128)S(1)} async-done(((f32[16,2,8]{2,1,0:T(2,128)}), f32[16,2,8]{2,1,0:T(2,128)S(1)}, u32[]{:S(2)}, u32[]{:S(2)}) %all-to-all-start.7) | async-done | bytes 1056 | tf_op jit(solution)/shard_map/all_to_all | solution.py:132
  260.9 9.8 %all_to_all.46 = bf16[16,2,8]{2,1,0:T(2,128)(2,1)S(1)} all-to-all(bf16[16,2,8]{2,1,0:T(2,128)(2,1)S(1)} %copy.112), channel_id=1, replica_groups=mesh['node'=16,'local'=64] {'node'}, dimensions={0} | all-to-all | bytes 1024 | tf_op jit(solution)/shard_map/all_to_all | solution.py:47
  271.0 14.6 %all_to_all.47 = bf16[64,1,16]{2,1,0:T(2,128)(2,1)S(1)} all-to-all(bf16[64,1,16]{2,1,0:T(2,128)(2,1)S(1)} %copy.114), channel_id=1, replica_groups=mesh['node'=16,'local'=64] {'local'}, dimensions={0} | all-to-all | bytes 4096 | tf_op jit(solution)/shard_map/all_to_all | solution.py:90
  285.8 1.4 fusion.20
  (64 shorter events, 14.9 us)
Async XLA Ops:
  0.6 111.0 %copy-start = (bf16[1,1024,896]{2,1,0:T(8,128)(2,1)S(1)}, bf16[1,1024,896]{2,1,0:T(8,128)(2,1)}, u32[]{:S(2)}) copy-start(bf16[1,1024,896]{2,1,0:T(8,128)(2,1)} %param.9) | copy-start | bytes 5505028
  3.1 24.8 %all-to-all-start = ((s32[16,2,8]{2,1,0:T(2,128)}), s32[16,2,8]{2,1,0:T(2,128)S(1)}, u32[]{:S(2)}, u32[]{:S(2)}) async-start(s32[16,2,8]{2,1,0:T(2,128)} %copy.107), calls=%async_computation | async-start | bytes 32768 | tf_op jit(solution)/shard_map/all_to_all | solution.py:46
  27.9 19.7 %all-to-all-start.3 = ((bf16[16,2,7168]{2,1,0:T(2,128)(2,1)}), bf16[16,2,7168]{2,1,0:T(2,128)(2,1)S(1)}, u32[]{:S(2)}, u32[]{:S(2)}) async-start(bf16[16,2,7168]{2,1,0:T(2,128)(2,1)} %copy.115), calls=%async_computation.3 | async-start | bytes 917504 | tf_op jit(solution)/shard_map/all_to_all | solution.py:45
  50.0 61.7 %all-to-all-start.4 = ((bf16[64,16,896]{2,1,0:T(8,128)(2,1)}), bf16[64,16,896]{2,1,0:T(8,128)(2,1)}, u32[]{:S(2)}, u32[]{:S(2)}) async-start(bf16[64,16,896]{2,1,0:T(8,128)(2,1)} %bitcast.79), calls=%async_computation.4 | async-start | bytes 3670016 | tf_op jit(solution)/shard_map/all_to_all | solution.py:89
  126.9 41.3 %collective-permute-start = (bf16[1024,1,2,2,128]{4,0,3,2,1:T(8,128)(2,1)}, bf16[1024,1,2,2,128]{4,0,3,2,1:T(8,128)(2,1)S(1)}, u32[]{:S(2)}, u32[]{:S(2)}) collective-permute-start(bf16[1024,1,2,2,128]{4,0,3,2,1:T(8,128)(2,1)} %copy.133), channel_id=1, source_target_pairs={{0,4},{1,5},{2,6},{3,7},{4,0},{5,1},{6,2},{7,3},{8,12},{9,13},{10,... | collective-permute-start | bytes 3145736 | tf_op jit(solution)/shard_map/ppermute | solution.py:10
  168.4 49.9 %copy-start.1 = (bf16[1,1024,128]{2,1,0:T(8,128)(2,1)S(1)}, bf16[1,1024,128]{2,1,0:T(8,128)(2,1)}, u32[]{:S(2)}) copy-start(bf16[1,1024,128]{2,1,0:T(8,128)(2,1)} %param.10) | copy-start | bytes 786436
  168.4 49.9 %copy-start.2 = (bf16[1,1024,128]{2,1,0:T(8,128)(2,1)S(1)}, bf16[1,1024,128]{2,1,0:T(8,128)(2,1)}, u32[]{:S(2)}) copy-start(bf16[1,1024,128]{2,1,0:T(8,128)(2,1)} %param.11) | copy-start | bytes 786436
  168.5 37.7 %collective-permute-start.1 = (bf16[1024,1,1,2,128]{4,0,3,2,1:T(8,128)(2,1)S(1)}, bf16[1024,1,1,2,128]{4,0,3,2,1:T(8,128)(2,1)S(1)}, u32[]{:S(2)}, u32[]{:S(2)}) collective-permute-start(bf16[1024,1,1,2,128]{4,0,3,2,1:T(8,128)(2,1)S(1)} %dynamic-slice_convert_fusion), channel_id=1, source_target_pairs={{0,2},{1,3},{2,0},{3,1},{4,6},{5,7},{6,4},{7,5},{8,10},{9,11},{10,... | collective-permute-start | bytes 1572872 | tf_op jit(solution)/shard_map/ppermute | solution.py:10
  206.3 46.3 %copy-start.3 = (bf16[8,8]{1,0:T(8,128)(2,1)S(1)}, bf16[8,8]{1,0:T(8,128)(2,1)}, u32[]{:S(2)}) copy-start(bf16[8,8]{1,0:T(8,128)(2,1)} %param.8) | copy-start | bytes 388
  207.1 11.2 %collective-permute-start.2 = (bf16[1024,1,1,1,128]{4,0,3,2,1:T(8,128)(2,1)}, bf16[1024,1,1,1,128]{4,0,3,2,1:T(8,128)(2,1)}, u32[]{:S(2)}, u32[]{:S(2)}) collective-permute-start(bf16[1024,1,1,1,128]{4,0,3,2,1:T(8,128)(2,1)} %dynamic-slice_convert_fusion.1), channel_id=1, source_target_pairs={{0,1},{1,0},{2,3},{3,2},{4,5},{5,4},{6,7},{7,6},{8,9},{9,8},{10,11... | collective-permute-start | bytes 786440 | tf_op jit(solution)/shard_map/ppermute | solution.py:10
  211.1 18.0 %all-to-all-start.5 = ((s32[64,1,16]{2,1,0:T(1,128)}), s32[64,1,16]{2,1,0:T(1,128)S(1)}, u32[]{:S(2)}, u32[]{:S(2)}) async-start(s32[64,1,16]{2,1,0:T(1,128)} %bitcast.19), calls=%async_computation.5 | async-start | bytes 65536 | tf_op jit(solution)/shard_map/all_to_all | solution.py:91
  245.7 14.3 %all-to-all-start.7 = ((f32[16,2,8]{2,1,0:T(2,128)}), f32[16,2,8]{2,1,0:T(2,128)S(1)}, u32[]{:S(2)}, u32[]{:S(2)}) async-start(f32[16,2,8]{2,1,0:T(2,128)} %copy.122), calls=%async_computation.7 | async-start | bytes 32768 | tf_op jit(solution)/shard_map/all_to_all | solution.py:132
where the time goes:
time: 289 us; the launch traced here: 288 us
  waiting for transfers between devices  140 us (48%)
  starting transfers between devices  73.9 us (26%)
  blocking collectives  39.1 us (14%)
  local copies, waits for them, and re-layouts  19.6 us (7%)
  other arithmetic  7.47 us (3%)
  matrix products  7.02 us (2%)
    ppermute x3, waiting for transfers between devices, partner(): lax.ppermute(x, axis, [(i, i ^ 1 << apart) for i in range(lax.axis_size(a...  55.1 us
    all_to_all x1, waiting for transfers between devices, body(): lax.all_to_all(spread_rows, 'local', split_axis=0, concat_axis=0, tiled=T...  47.5 us
    ppermute x3, starting transfers between devices, partner(): lax.ppermute(x, axis, [(i, i ^ 1 << apart) for i in range(lax.axis_size(a...  24.5 us
    all_to_all x1, starting transfers between devices, body(): lax.all_to_all(send_ids, 'node', split_axis=0, concat_axis=0, tiled=True)  17.4 us
    all_to_all x1, waiting for transfers between devices, body(): lax.all_to_all(send_rows, 'node', split_axis=0, concat_axis=0, tiled=True)  15.6 us
    all_to_all x1, blocking collectives, body(): lax.all_to_all(returned.astype(jnp.bfloat16), 'local', split_axis=0, conc...  14.6 us
    all_to_all x1, blocking collectives, body(): lax.all_to_all(wide_weight, 'local', split_axis=0, concat_axis=0, tiled=T...  14.6 us
    all_to_all x1, starting transfers between devices, body(): lax.all_to_all(spread_rows, 'local', split_axis=0, concat_axis=0, tiled=T...  14.1 us
  transfers between devices with their start and end apart: 8, of which 7 were waited for; matrix products, arithmetic and copies ran while one was open for 3% of the time, Pallas kernels for 0%

commit v1 on v0

v1 whole, which is shorter than its diff:
```python
import functools

import jax
import jax.numpy as jnp
from jax import lax
from jax.experimental import pallas as pl
from jax.experimental.pallas import tpu as pltpu
from jax.sharding import Mesh
from jax.sharding import PartitionSpec as P

EPG = 8
LANES = 128
F32 = jnp.float32
BF16 = jnp.bfloat16


def pick_kernel(lines_ref, rows_ref, out_ref, slot_weight_ref):
    expert = pl.program_id(0)
    experts = lines_ref.shape[0] // 2
    lines = lines_ref[...]
    line = lax.broadcasted_iota(jnp.int32, lines.shape, 0)
    slot_of = jnp.sum(jnp.where(line == expert, lines, 0.0), axis=0, keepdims=True)
    weight_of = jnp.sum(jnp.where(line == expert + experts, lines, 0.0), axis=0, keepdims=True)
    _, slots, _ = out_ref.shape
    slot = lax.broadcasted_iota(jnp.int32, (slots, lines.shape[1]), 0).astype(F32)
    holds = jnp.where(slot_of == slot, 1.0, 0.0).astype(BF16)
    out_ref[0] = jnp.dot(holds, rows_ref[...], preferred_element_type=F32).astype(BF16)
    weights = jnp.broadcast_to(weight_of, (8, lines.shape[1])).astype(BF16)
    slot_weight_ref[0] = lax.dot_general(
        weights, holds, (((1,), (1,)), ((), ())), preferred_element_type=F32
    )[:1]


def pick(lines, rows, slots):
    experts = lines.shape[0] // 2
    row_count, width = rows.shape
    return pl.pallas_call(
        pick_kernel,
        grid=(experts,),
        in_specs=[
            pl.BlockSpec(lines.shape, lambda e: (0, 0)),
            pl.BlockSpec(rows.shape, lambda e: (0, 0)),
        ],
        out_specs=[
            pl.BlockSpec((1, slots, width), lambda e: (e, 0, 0)),
            pl.BlockSpec((1, 1, slots), lambda e: (e, 0, 0)),
        ],
        out_shape=[
            jax.ShapeDtypeStruct((experts, slots, width), BF16),
            jax.ShapeDtypeStruct((experts, 1, slots), F32),
        ],
        compiler_params=pltpu.CompilerParams(vmem_limit_bytes=32 * 1024 * 1024),
        cost_estimate=pl.CostEstimate(
            flops=2 * experts * slots * row_count * width, bytes_accessed=2_500_000, transcendentals=0
        ),
    )(lines, rows)


def as_line(column):
    count = column.shape[0]
    same = lax.broadcasted_iota(jnp.int32, (count, count), 0) == lax.broadcasted_iota(
        jnp.int32, (count, count), 1
    )
    return jnp.sum(jnp.where(same, column, 0.0), axis=0, keepdims=True)


def as_column(line):
    count = line.shape[1]
    same = lax.broadcasted_iota(jnp.int32, (count, count), 0) == lax.broadcasted_iota(
        jnp.int32, (count, count), 1
    )
    return jnp.sum(jnp.where(same, line, 0.0), axis=1, keepdims=True)


def product_kernel(rows_ref, weight_ref, hidden_ref, out_ref, dot_ref):
    rows = rows_ref[0]
    blocks, slots, width = out_ref.shape
    total = jnp.zeros((slots, width), F32)
    for block in range(blocks):
        term = lax.dot_general(
            rows,
            weight_ref[0, block * width : (block + 1) * width, :],
            (((1,), (1,)), ((), ())),
            preferred_element_type=F32,
        ).astype(BF16)
        out_ref[block] = term
        total += term.astype(F32) * hidden_ref[block].astype(F32)
    dot_ref[0] = as_line(jnp.sum(total, axis=1, keepdims=True))


def product(rows, weight, hidden):
    z_count, slots, width = rows.shape
    blocks, _, lanes = hidden.shape
    units = weight.shape[1]
    return pl.pallas_call(
        product_kernel,
        grid=(z_count,),
        in_specs=[
            pl.BlockSpec((1, slots, width), lambda z: (z, 0, 0)),
            pl.BlockSpec((1, units, width), lambda z: (0, 0, 0)),
            pl.BlockSpec((blocks, slots, lanes), lambda z: (0, z, 0)),
        ],
        out_specs=[
            pl.BlockSpec((blocks, slots, lanes), lambda z: (0, z, 0)),
            pl.BlockSpec((1, 1, slots), lambda z: (z, 0, 0)),
        ],
        out_shape=[
            jax.ShapeDtypeStruct((blocks, z_count * slots, lanes), BF16),
            jax.ShapeDtypeStruct((z_count, 1, slots), F32),
        ],
        compiler_params=pltpu.CompilerParams(vmem_limit_bytes=32 * 1024 * 1024),
        cost_estimate=pl.CostEstimate(
            flops=2 * z_count * slots * width * units, bytes_accessed=8_000_000, transcendentals=0
        ),
    )(rows, weight, hidden)


def gate_kernel(u_ref, gate_ref, up_ref, weight_ref, grad_ref):
    u = u_ref[...].astype(F32)
    a = gate_ref[0].astype(F32)
    b = up_ref[0].astype(F32)
    s = 1.0 / (1.0 + jnp.exp(-a))
    scaled = as_column(weight_ref[0]) * u
    grad_ref[0, 0] = (scaled * b * s * (1.0 + a * (1.0 - s))).astype(BF16)
    grad_ref[0, 1] = (scaled * a * s).astype(BF16)


def gate(u, gate_pre, up_pre, slot_weight):
    z_count, _, slots = slot_weight.shape
    slot_count, width = u.shape
    return pl.pallas_call(
        gate_kernel,
        grid=(z_count,),
        in_specs=[
            pl.BlockSpec((slots, width), lambda z: (z, 0)),
            pl.BlockSpec((1, slots, width), lambda z: (0, z, 0)),
            pl.BlockSpec((1, slots, width), lambda z: (0, z, 0)),
            pl.BlockSpec((1, 1, slots), lambda z: (z, 0, 0)),
        ],
        out_specs=pl.BlockSpec((1, 2, slots, width), lambda z: (0, 0, z, 0)),
        out_shape=jax.ShapeDtypeStruct((1, 2, slot_count, width), BF16),
        compiler_params=pltpu.CompilerParams(vmem_limit_bytes=32 * 1024 * 1024),
        cost_estimate=pl.CostEstimate(
            flops=20 * slot_count * width, bytes_accessed=2_000_000, transcendentals=slot_count * width
        ),
    )(u, gate_pre, up_pre, slot_weight)


def body(out_grad, expert_ids, route_weights, down_weight, gate_pre, up_pre):
    n_node = lax.axis_size("node")
    n_z = lax.axis_size("z")
    n_x = lax.axis_size("x")
    tok_dev, model_width = out_grad.shape
    top_count = expert_ids.shape[1]
    width = model_width // n_x
    cap_group = 4 * tok_dev // n_node
    cap_expert = 2 * tok_dev
    slots = n_x * cap_expert
    row_count = n_node * n_x * cap_group
    tiles = width // LANES

    a = gate_pre[0].astype(F32)
    hidden = (a * (1.0 / (1.0 + jnp.exp(-a))) * up_pre[0].astype(F32)).astype(BF16)
    hidden_all = lax.all_gather(hidden, "x", tiled=True).reshape(n_x, hidden.shape[0], LANES)

    group_iota = jnp.arange(n_node, dtype=jnp.int32)
    reaches = jnp.any((expert_ids // n_z)[:, :, None] == group_iota, axis=1).astype(jnp.int32)
    order_in = jnp.cumsum(reaches, axis=0) - reaches
    chosen = (
        (reaches.T[:, None, :] == 1)
        & (order_in.T[:, None, :] == jnp.arange(cap_group, dtype=jnp.int32)[None, :, None])
    ).astype(BF16)
    named = jnp.concatenate([expert_ids.astype(BF16), route_weights], axis=1)
    source = jnp.concatenate([out_grad, jnp.pad(named, ((0, 0), (0, LANES - 2 * top_count)))], axis=1)
    send = jnp.einsum("gkt,td->gkd", chosen, source, preferred_element_type=F32).astype(BF16)
    send = send.reshape(n_node, cap_group, n_x * tiles + 1, LANES)
    data = send[:, :, : n_x * tiles].reshape(n_node, cap_group, n_x, tiles, LANES)
    tail = jnp.broadcast_to(send[:, :, None, n_x * tiles :], (n_node, cap_group, n_x, 1, LANES))
    send = jnp.concatenate([data, tail], axis=3).transpose(0, 2, 1, 3, 4)
    send = send.reshape(n_node * n_x, cap_group * (tiles + 1), LANES)
    got = lax.all_to_all(send, ("node", "x"), split_axis=0, concat_axis=0, tiled=True)
    got = got.reshape(row_count, tiles + 1, LANES)

    rows = got[:, :tiles].reshape(row_count, width)
    ids = got[:, tiles, :top_count].astype(F32).astype(jnp.int32)
    weights = got[:, tiles, top_count : 2 * top_count].astype(F32)
    my_group = lax.axis_index("node")
    member = (ids - my_group * n_z)[:, None, :] == jnp.arange(n_z, dtype=jnp.int32)[None, :, None]
    named_by = jnp.any(member, axis=2)
    weight_each = jnp.sum(jnp.where(member, weights[:, None, :], 0.0), axis=2)
    row = jnp.arange(row_count, dtype=jnp.int32)
    relay = row // cap_group % n_x
    earlier = (row[None, :] < row[:, None]) & (relay[None, :] == relay[:, None])
    place = jnp.dot(earlier.astype(BF16), named_by.astype(BF16), preferred_element_type=F32)
    slot_each = jnp.where(named_by, (relay * cap_expert).astype(F32)[:, None] + place, -1.0)
    lines = jnp.concatenate([slot_each.T, weight_each.T], axis=0)
    picked, slot_weight = pick(lines, rows, slots)
    taken = lax.all_to_all(picked, "z", split_axis=0, concat_axis=0, tiled=True)

    partial, dots = product(taken, down_weight, hidden_all)
    u = lax.psum_scatter(
        partial.reshape(n_x * n_z * slots, LANES), "x", scatter_dimension=0, tiled=True
    )

    both = jnp.concatenate([dots, slot_weight], axis=1)
    both = lax.all_to_all(both, "z", split_axis=0, concat_axis=0, tiled=True)
    dots = both[:, 0]
    grad_pre = gate(u, gate_pre, up_pre, both[:, 1:])
    slot_iota = jnp.arange(slots, dtype=jnp.int32).astype(F32)
    value = jnp.sum(
        jnp.where(slot_each[:, :, None] == slot_iota, dots[None], 0.0), axis=2
    )
    value = jnp.sum(jnp.where(member, value[:, :, None], 0.0), axis=1)
    value = value.reshape(n_node * n_x, cap_group, top_count)
    back = lax.all_to_all(value, ("node", "x"), split_axis=0, concat_axis=0, tiled=True)
    back = jnp.sum(back.reshape(n_node, n_x, cap_group, top_count), axis=1)
    grad_weights = jnp.sum(chosen.astype(F32)[..., None] * back[:, :, None, :], axis=(0, 1))
    return (grad_pre, grad_weights)


def solution(mesh):
    devices = mesh.devices
    n_node, n_local = devices.shape
    split = Mesh(devices.reshape(n_node, EPG, n_local // EPG), ("node", "z", "x"))
    first = ("node", "z", "x")
    return jax.shard_map(
        body,
        mesh=split,
        in_specs=(
            P(first, None),
            P(first, None),
            P(first, None),
            P(first, None, None),
            P(first, None, None),
            P(first, None, None),
        ),
        out_specs=(P(first, None, None, None), P(first, None)),
        check_vma=False,
    )
```

time: 289 us -> 173 us (0.60)
  the two profiles are of different devices: /device:TPU:1 before, /device:TPU:6 now
where the time goes in v1:
time: 173 us
  waiting for transfers between devices  89 us (51%)
  starting transfers between devices  41.8 us (24%)
  between operations  14.3 us (8%)
  Pallas kernels  12.6 us (7%)
  local copies, waits for them, and re-layouts  8.33 us (5%)
  other arithmetic  5.11 us (3%)
    all_to_all x1, waiting for transfers between devices, body(): taken = lax.all_to_all(picked, 'z', split_axis=0, concat_axis=0, tiled=True)  25.8 us
    all_gather x1, waiting for transfers between devices, body(): lax.all_gather(hidden, 'x', tiled=True).reshape(n_x, hidden.shape[0], LANES)  20 us
    all_to_all x1, starting transfers between devices, body(): lax.all_to_all(send, ('node', 'x'), split_axis=0, concat_axis=0, tiled=True)  18.3 us
    all_to_all x1, waiting for transfers between devices, body(): lax.all_to_all(send, ('node', 'x'), split_axis=0, concat_axis=0, tiled=True)  17.5 us
    all_to_all x1, starting transfers between devices, body(): taken = lax.all_to_all(picked, 'z', split_axis=0, concat_axis=0, tiled=True)  12.5 us
    all_to_all x1, waiting for transfers between devices, body(): lax.all_to_all(value, ('node', 'x'), split_axis=0, concat_axis=0, tiled=T...  12.1 us
    pallas_call x1, Pallas kernels, product(): pl.pallas_call(product_kernel, grid=(z_count,), in_specs=[pl.BlockSpec((1...  7.64 us
    all_to_all x1, waiting for transfers between devices, body(): both = lax.all_to_all(both, 'z', split_axis=0, concat_axis=0, tiled=True)  7.53 us
  transfers between devices with their start and end apart: 6, of which 6 were waited for; matrix products, arithmetic and copies ran while one was open for 3% of the time, Pallas kernels for 1%

profile of v1, /device:TPU:6, one launch (start us, length us, event | category | flops | bytes accessed | tf_op | source)
XLA Modules:
  0.0 172.6 jit_solution(18420803609423732737)
XLA Ops:
  7.2 0.8 add_select_fusion
  8.1 0.8 fusion.27
  8.8 1.2 convolution_convert_fusion
  10.5 0.9 copy.32
  11.5 18.3 %all-to-all-start = ((bf16[128,16,128]{2,1,0:T(8,128)(2,1)}), bf16[128,16,128]{2,1,0:T(8,128)(2,1)S(1)}, u32[]{:S(2)}, u32[]{:S(2)}) async-start(bf16[128,16,128]{2,1,0:T(8,128)(2,1)} %bitcast.5), calls=%async_computation | async-start | bytes 1048576 | tf_op jit(solution)/shard_map/all_to_all | solution.py:181
  29.9 0.9 fusion.5
  30.8 17.5 %all-to-all-done = bf16[128,16,128]{2,1,0:T(8,128)(2,1)S(1)} async-done(((bf16[128,16,128]{2,1,0:T(8,128)(2,1)}), bf16[128,16,128]{2,1,0:T(8,128)(2,1)S(1)}, u32[]{:S(2)}, u32[]{:S(2)}) %all-to-all-start) | async-done | bytes 524320 | tf_op jit(solution)/shard_map/all_to_all | solution.py:181
  49.8 2.0 %shard_map.77 = (bf16[8,128,896]{2,1,0:T(8,128)(2,1)S(1)}, f32[8,1,128]{2,1,0:T(1,128)S(1)}) custom-call(f32[16,256]{1,0:T(8,128)S(1)} %pad_maximum_fusion.lines_ref, bf16[256,896]{1,0:T(8,128)(2,1)S(1)} %copy.36.rows_ref), custom_call_target="tpu_custom_call" | custom-call | flops 469762048 | bytes 2500000 | tf_op jit(solution)/shard_map/pallas_call | solution.py:37
  51.8 1.2 copy-done
  53.0 12.5 %all-to-all-start.1 = ((bf16[8,128,896]{2,1,0:T(8,128)(2,1)}), bf16[8,128,896]{2,1,0:T(8,128)(2,1)S(1)}, u32[]{:S(2)}, u32[]{:S(2)}) async-start(bf16[8,128,896]{2,1,0:T(8,128)(2,1)} %copy-done), calls=%async_computation.1 | async-start | bytes 3670016 | tf_op jit(solution)/shard_map/all_to_all | solution.py:198
  65.6 20.0 %all-gather.2.cloned.1.call-done = bf16[8192,128]{1,0:T(8,128)(2,1)} async-done(((bf16[1024,128]{1,0:T(8,128)(2,1)}), bf16[8192,128]{1,0:T(8,128)(2,1)}) %all-gather.2.cloned.1.call-update) | async-done | bytes 2097168 | tf_op jit(solution)/shard_map/all_gather | solution.py:164
  85.6 25.8 %all-to-all-done.1.rows_ref = bf16[8,128,896]{2,1,0:T(8,128)(2,1)S(1)} async-done(((bf16[8,128,896]{2,1,0:T(8,128)(2,1)}), bf16[8,128,896]{2,1,0:T(8,128)(2,1)S(1)}, u32[]{:S(2)}, u32[]{:S(2)}) %all-to-all-start.1) | async-done | bytes 1835040 | tf_op jit(solution)/shard_map/all_to_all | solution.py:198
  111.4 1.6 copy-done.4
  113.0 1.5 copy-done.5
  114.5 7.6 %shard_map.78 = (bf16[8,1024,128]{2,1,0:T(8,128)(2,1)}, f32[8,1,128]{2,1,0:T(1,128)S(1)}) custom-call(bf16[8,128,896]{2,1,0:T(8,128)(2,1)S(1)} %all-to-all-done.1.rows_ref, bf16[1,1024,896]{2,1,0:T(8,128)(2,1)S(1)} %copy-done.5, bf16[8,1024,128]{2,1,0:T(8,128)(2,1)S(1)} %bitcast.36), custom_call_target="tpu_custom_call" | custom-call | flops 1879048192 | bytes 8000000 | tf_op jit(solution)/shard_map/pallas_call | solution.py:95
  122.8 3.3 %all-to-all-start.2 = ((f32[8,2,128]{2,1,0:T(2,128)}), f32[8,2,128]{2,1,0:T(2,128)S(1)}, u32[]{:S(2)}, u32[]{:S(2)}) async-start(f32[8,2,128]{2,1,0:T(2,128)} %pad_maximum_fusion.1), calls=%async_computation.3 | async-start | bytes 16384 | tf_op jit(solution)/shard_map/all_to_all | solution.py:206
  126.3 7.5 %all-to-all-done.2 = f32[8,2,128]{2,1,0:T(2,128)S(1)} async-done(((f32[8,2,128]{2,1,0:T(2,128)}), f32[8,2,128]{2,1,0:T(2,128)S(1)}, u32[]{:S(2)}, u32[]{:S(2)}) %all-to-all-start.2) | async-done | bytes 8224 | tf_op jit(solution)/shard_map/all_to_all | solution.py:206
  134.5 0.8 copy.39
  135.3 7.5 %all-to-all-start.3 = ((f32[128,2,8]{2,1,0:T(2,128)}), f32[128,2,8]{2,1,0:T(2,128)S(1)}, u32[]{:S(2)}, u32[]{:S(2)}) async-start(f32[128,2,8]{2,1,0:T(2,128)} %bitcast.18), calls=%async_computation.4 | async-start | bytes 262144 | tf_op jit(solution)/shard_map/all_to_all | solution.py:215
  142.9 12.1 %all-to-all-done.3 = f32[128,2,8]{2,1,0:T(2,128)S(1)} async-done(((f32[128,2,8]{2,1,0:T(2,128)}), f32[128,2,8]{2,1,0:T(2,128)S(1)}, u32[]{:S(2)}, u32[]{:S(2)}) %all-to-all-start.3) | async-done | bytes 8224 | tf_op jit(solution)/shard_map/all_to_all | solution.py:215
  155.1 0.7 multiply_reduce_fusion
  155.8 6.0 %reduce-scatter.2.cloned.1.call-done.u_ref = bf16[1024,128]{1,0:T(8,128)(2,1)} async-done(((bf16[8192,128]{1,0:T(8,128)(2,1)}), bf16[1024,128]{1,0:T(8,128)(2,1)}) %reduce-scatter.2.cloned.1.call-update) | async-done | bytes 262160 | tf_op jit(solution)/shard_map/reduce_scatter | solution.py:201
  161.8 0.9 copy-done.3
  162.7 3.0 %shard_map.79 = bf16[1,2,1024,128]{3,2,1,0:T(8,128)(2,1)} custom-call(bf16[1024,128]{1,0:T(8,128)(2,1)S(1)} %copy-done.3, bf16[1,1024,128]{2,1,0:T(8,128)(2,1)S(1)} %copy-done.2, bf16[1,1024,128]{2,1,0:T(8,128)(2,1)S(1)} %copy-done.1, f32[8,1,128]{2,1,0:T(1,128)S(1)} %get-tuple-element.11.weight_ref), custom_call_target="tpu_custom_call" | custom-call | flops 2621440 | bytes 2000000 | tf_op jit(solution)/shard_map/pallas_call | solution.py:131
  (44 shorter events, 3.7 us)
Async XLA Ops:
  10.4 19.4 %copy-start.1 = (bf16[1,1024,128]{2,1,0:T(8,128)(2,1)S(1)}, bf16[1,1024,128]{2,1,0:T(8,128)(2,1)}, u32[]{:S(2)}) copy-start(bf16[1,1024,128]{2,1,0:T(8,128)(2,1)} %up_ref.1) | copy-start | bytes 786436
  10.4 19.4 %copy-start.2 = (bf16[1,1024,128]{2,1,0:T(8,128)(2,1)S(1)}, bf16[1,1024,128]{2,1,0:T(8,128)(2,1)}, u32[]{:S(2)}) copy-start(bf16[1,1024,128]{2,1,0:T(8,128)(2,1)} %gate_ref.1) | copy-start | bytes 786436
  11.5 36.8 %all-to-all-start = ((bf16[128,16,128]{2,1,0:T(8,128)(2,1)}), bf16[128,16,128]{2,1,0:T(8,128)(2,1)S(1)}, u32[]{:S(2)}, u32[]{:S(2)}) async-start(bf16[128,16,128]{2,1,0:T(8,128)(2,1)} %bitcast.5), calls=%async_computation | async-start | bytes 1048576 | tf_op jit(solution)/shard_map/all_to_all | solution.py:181
  29.8 55.8 %all-gather.2.cloned.1.call-start = ((), (), s32[]{:S(2)}) async-start(), calls=%async_computation.5 | async-start | bytes 2359296 | tf_op jit(solution)/shard_map/all_gather | solution.py:164
  51.8 1.2 copy-start
  53.0 58.4 %all-to-all-start.1 = ((bf16[8,128,896]{2,1,0:T(8,128)(2,1)}), bf16[8,128,896]{2,1,0:T(8,128)(2,1)S(1)}, u32[]{:S(2)}, u32[]{:S(2)}) async-start(bf16[8,128,896]{2,1,0:T(8,128)(2,1)} %copy-done), calls=%async_computation.1 | async-start | bytes 3670016 | tf_op jit(solution)/shard_map/all_to_all | solution.py:198
  65.6 96.2 %reduce-scatter.2.cloned.1.call-start = ((), (), s32[]{:S(2)}) async-start(), calls=%async_computation.6 | async-start | bytes 2359296 | tf_op jit(solution)/shard_map/reduce_scatter | solution.py:201
  111.4 1.6 copy-start.4
  113.0 1.5 copy-start.5
  122.8 11.0 %all-to-all-start.2 = ((f32[8,2,128]{2,1,0:T(2,128)}), f32[8,2,128]{2,1,0:T(2,128)S(1)}, u32[]{:S(2)}, u32[]{:S(2)}) async-start(f32[8,2,128]{2,1,0:T(2,128)} %pad_maximum_fusion.1), calls=%async_computation.3 | async-start | bytes 16384 | tf_op jit(solution)/shard_map/all_to_all | solution.py:206
  135.3 19.6 %all-to-all-start.3 = ((f32[128,2,8]{2,1,0:T(2,128)}), f32[128,2,8]{2,1,0:T(2,128)S(1)}, u32[]{:S(2)}, u32[]{:S(2)}) async-start(f32[128,2,8]{2,1,0:T(2,128)} %bitcast.18), calls=%async_computation.4 | async-start | bytes 262144 | tf_op jit(solution)/shard_map/all_to_all | solution.py:215
  161.8 0.9 copy-start.3
Sparse Core Ops, SparseCore 0:
  33.3 52.2 all-gather.1
  122.3 39.4 reduce-scatter.1

commit v2 on v1

--- a/solution.py
+++ b/solution.py
@@ -49,7 +49,7 @@
             jax.ShapeDtypeStruct((experts, slots, width), BF16),
             jax.ShapeDtypeStruct((experts, 1, slots), F32),
         ],
-        compiler_params=pltpu.CompilerParams(vmem_limit_bytes=32 * 1024 * 1024),
+        compiler_params=pltpu.CompilerParams(vmem_limit_bytes=60 * 1024 * 1024),
         cost_estimate=pl.CostEstimate(
             flops=2 * experts * slots * row_count * width, bytes_accessed=2_500_000, transcendentals=0
         ),
@@ -72,45 +72,52 @@
     return jnp.sum(jnp.where(same, line, 0.0), axis=1, keepdims=True)
 
 
-def product_kernel(rows_ref, weight_ref, hidden_ref, out_ref, dot_ref):
-    rows = rows_ref[0]
-    blocks, slots, width = out_ref.shape
-    total = jnp.zeros((slots, width), F32)
-    for block in range(blocks):
-        term = lax.dot_general(
-            rows,
-            weight_ref[0, block * width : (block + 1) * width, :],
-            (((1,), (1,)), ((), ())),
-            preferred_element_type=F32,
-        ).astype(BF16)
-        out_ref[block] = term
-        total += term.astype(F32) * hidden_ref[block].astype(F32)
-    dot_ref[0] = as_line(jnp.sum(total, axis=1, keepdims=True))
+def product_kernel(rows_ref, weight_ref, hidden_ref, out_ref, dot_ref, total):
+    step = pl.program_id(0)
+    z_count, slots, width = rows_ref.shape
+    rows = rows_ref[...].reshape(z_count * slots, width)
+    term = lax.dot_general(
+        rows, weight_ref[0], (((1,), (1,)), ((), ())), preferred_element_type=F32
+    ).astype(BF16)
+    dots = jnp.where(step == 0, 0.0, total[...])
+    for block in range(out_ref.shape[0]):
+        part = term[:, block * LANES : (block + 1) * LANES]
+        out_ref[block] = part
+        dots += part.astype(F32) * hidden_ref[block].astype(F32)
+    total[...] = dots
+
+    @pl.when(step == pl.num_programs(0) - 1)
+    def _():
+        for z in range(z_count):
+            summed = jnp.sum(total[z * slots : (z + 1) * slots, :], axis=1, keepdims=True)
+            dot_ref[z] = as_line(summed)
 
 
 def product(rows, weight, hidden):
     z_count, slots, width = rows.shape
-    blocks, _, lanes = hidden.shape
+    blocks, slot_count, lanes = hidden.shape
     units = weight.shape[1]
+    per_step = 2
     return pl.pallas_call(
         product_kernel,
-        grid=(z_count,),
+        grid=(blocks // per_step,),
         in_specs=[
-            pl.BlockSpec((1, slots, width), lambda z: (z, 0, 0)),
-            pl.BlockSpec((1, units, width), lambda z: (0, 0, 0)),
-            pl.BlockSpec((blocks, slots, lanes), lambda z: (0, z, 0)),
+            pl.BlockSpec((z_count, slots, width), lambda i: (0, 0, 0)),
+            pl.BlockSpec((1, per_step * lanes, width), lambda i: (0, i, 0)),
+            pl.BlockSpec((per_step, slot_count, lanes), lambda i: (i, 0, 0)),
         ],
         out_specs=[
-            pl.BlockSpec((blocks, slots, lanes), lambda z: (0, z, 0)),
-            pl.BlockSpec((1, 1, slots), lambda z: (z, 0, 0)),
+            pl.BlockSpec((per_step, slot_count, lanes), lambda i: (i, 0, 0)),
+            pl.BlockSpec((z_count, 1, slots), lambda i: (0, 0, 0)),
         ],
         out_shape=[
-            jax.ShapeDtypeStruct((blocks, z_count * slots, lanes), BF16),
+            jax.ShapeDtypeStruct((blocks, slot_count, lanes), BF16),
             jax.ShapeDtypeStruct((z_count, 1, slots), F32),
         ],
-        compiler_params=pltpu.CompilerParams(vmem_limit_bytes=32 * 1024 * 1024),
+        scratch_shapes=[pltpu.VMEM((slot_count, lanes), F32)],
+        compiler_params=pltpu.CompilerParams(vmem_limit_bytes=52 * 1024 * 1024),
         cost_estimate=pl.CostEstimate(
-            flops=2 * z_count * slots * width * units, bytes_accessed=8_000_000, transcendentals=0
+            flops=2 * slot_count * width * units, bytes_accessed=8_000_000, transcendentals=0
         ),
     )(rows, weight, hidden)
 
@@ -120,7 +127,8 @@
     a = gate_ref[0].astype(F32)
     b = up_ref[0].astype(F32)
     s = 1.0 / (1.0 + jnp.exp(-a))
-    scaled = as_column(weight_ref[0]) * u
+    weight = jnp.concatenate([as_column(weight_ref[z]) for z in range(weight_ref.shape[0])], axis=0)
+    scaled = weight * u
     grad_ref[0, 0] = (scaled * b * s * (1.0 + a * (1.0 - s))).astype(BF16)
     grad_ref[0, 1] = (scaled * a * s).astype(BF16)
 
@@ -128,20 +136,22 @@
 def gate(u, gate_pre, up_pre, slot_weight):
     z_count, _, slots = slot_weight.shape
     slot_count, width = u.shape
+    per_step = z_count // 2
+    lines = per_step * slots
     return pl.pallas_call(
         gate_kernel,
-        grid=(z_count,),
+        grid=(2,),
         in_specs=[
-            pl.BlockSpec((slots, width), lambda z: (z, 0)),
-            pl.BlockSpec((1, slots, width), lambda z: (0, z, 0)),
-            pl.BlockSpec((1, slots, width), lambda z: (0, z, 0)),
-            pl.BlockSpec((1, 1, slots), lambda z: (z, 0, 0)),
-        ],
-        out_specs=pl.BlockSpec((1, 2, slots, width), lambda z: (0, 0, z, 0)),
+            pl.BlockSpec((lines, width), lambda z: (z, 0)),
+            pl.BlockSpec((1, lines, width), lambda z: (0, z, 0)),
+            pl.BlockSpec((1, lines, width), lambda z: (0, z, 0)),
+            pl.BlockSpec((per_step, 1, slots), lambda z: (z, 0, 0)),
+        ],
+        out_specs=pl.BlockSpec((1, 2, lines, width), lambda z: (0, 0, z, 0)),
         out_shape=jax.ShapeDtypeStruct((1, 2, slot_count, width), BF16),
-        compiler_params=pltpu.CompilerParams(vmem_limit_bytes=32 * 1024 * 1024),
+        compiler_params=pltpu.CompilerParams(vmem_limit_bytes=60 * 1024 * 1024),
         cost_estimate=pl.CostEstimate(
-            flops=20 * slot_count * width, bytes_accessed=2_000_000, transcendentals=slot_count * width
+            flops=30 * slot_count * width, bytes_accessed=2_000_000, transcendentals=slot_count * width
         ),
     )(u, gate_pre, up_pre, slot_weight)
 
@@ -161,6 +171,7 @@
 
     a = gate_pre[0].astype(F32)
     hidden = (a * (1.0 / (1.0 + jnp.exp(-a))) * up_pre[0].astype(F32)).astype(BF16)
+    hidden, expert_ids, route_weights = lax.optimization_barrier((hidden, expert_ids, route_weights))
     hidden_all = lax.all_gather(hidden, "x", tiled=True).reshape(n_x, hidden.shape[0], LANES)
 
     group_iota = jnp.arange(n_node, dtype=jnp.int32)

time: 173 us -> 171 us (0.988)
  the two profiles are of different devices: /device:TPU:6 before, /device:TPU:1 now
where the time goes in v2:
time: 171 us; the launch traced here: 169 us
  waiting for transfers between devices  85.5 us (50%)
  starting transfers between devices  42.8 us (25%)
  between operations  14.2 us (8%)
  Pallas kernels  13.3 us (8%)
  other arithmetic  6.75 us (4%)
  local copies, waits for them, and re-layouts  5.03 us (3%)
    all_to_all x1, waiting for transfers between devices, body(): taken = lax.all_to_all(picked, 'z', split_axis=0, concat_axis=0, tiled=True)  33.1 us
    all_to_all x1, starting transfers between devices, body(): lax.all_to_all(send, ('node', 'x'), split_axis=0, concat_axis=0, tiled=True)  19.4 us
    all_to_all x1, waiting for transfers between devices, body(): lax.all_to_all(send, ('node', 'x'), split_axis=0, concat_axis=0, tiled=True)  18.7 us
    all_to_all x1, waiting for transfers between devices, body(): lax.all_to_all(value, ('node', 'x'), split_axis=0, concat_axis=0, tiled=T...  13.7 us
    all_gather x1, waiting for transfers between devices, body(): lax.all_gather(hidden, 'x', tiled=True).reshape(n_x, hidden.shape[0], LANES)  12.9 us
    all_to_all x1, starting transfers between devices, body(): taken = lax.all_to_all(picked, 'z', split_axis=0, concat_axis=0, tiled=True)  12.3 us
    all_to_all x1, starting transfers between devices, body(): lax.all_to_all(value, ('node', 'x'), split_axis=0, concat_axis=0, tiled=T...  7.75 us
    all_to_all x1, waiting for transfers between devices, body(): both = lax.all_to_all(both, 'z', split_axis=0, concat_axis=0, tiled=True)  6.38 us
  transfers between devices with their start and end apart: 6, of which 5 were waited for; matrix products, arithmetic and copies ran while one was open for 4% of the time, Pallas kernels for 3%

profile of v2, /device:TPU:1, one launch (start us, length us, event | category | flops | bytes accessed | tf_op | source)
XLA Modules:
  0.0 169.1 jit_solution(6446135409054733490)
XLA Ops:
  7.2 1.9 %fusion.5 = bf16[1024,128]{1,0:T(8,128)(2,1)} fusion(bf16[1,1024,128]{2,1,0:T(8,128)(2,1)} %up_ref.1, bf16[1,1024,128]{2,1,0:T(8,128)(2,1)} %gate_ref.1), kind=kLoop, calls=%fused_computation.11 | loop fusion | flops 1048576 | bytes 786432 | tf_op jit(solution)/shard_map/convert_element_type | solution.py:173
  9.1 0.8 add_select_fusion
  10.0 0.8 fusion.27
  10.7 1.2 convolution_convert_fusion
  12.4 0.9 copy.32
  13.4 19.4 %all-to-all-start = ((bf16[128,16,128]{2,1,0:T(8,128)(2,1)}), bf16[128,16,128]{2,1,0:T(8,128)(2,1)S(1)}, u32[]{:S(2)}, u32[]{:S(2)}) async-start(bf16[128,16,128]{2,1,0:T(8,128)(2,1)} %bitcast.8), calls=%async_computation | async-start | bytes 1048576 | tf_op jit(solution)/shard_map/all_to_all | solution.py:192
  32.8 0.7 all-gather.2.cloned.1.call-update
  33.5 18.7 %all-to-all-done = bf16[128,16,128]{2,1,0:T(8,128)(2,1)S(1)} async-done(((bf16[128,16,128]{2,1,0:T(8,128)(2,1)}), bf16[128,16,128]{2,1,0:T(8,128)(2,1)S(1)}, u32[]{:S(2)}, u32[]{:S(2)}) %all-to-all-start) | async-done | bytes 524320 | tf_op jit(solution)/shard_map/all_to_all | solution.py:192
  53.1 1.0 copy.36.rows_ref
  54.4 0.6 pad_maximum_fusion.lines_ref
  55.0 5.0 %shard_map.77 = (bf16[8,128,896]{2,1,0:T(8,128)(2,1)}, f32[8,1,128]{2,1,0:T(1,128)}) custom-call(f32[16,256]{1,0:T(8,128)} %pad_maximum_fusion.lines_ref, bf16[256,896]{1,0:T(8,128)(2,1)} %copy.36.rows_ref), custom_call_target="tpu_custom_call" | custom-call | flops 469762048 | bytes 2500000 | tf_op jit(solution)/shard_map/pallas_call | solution.py:37
  60.0 12.3 %all-to-all-start.1 = ((bf16[8,128,896]{2,1,0:T(8,128)(2,1)}), bf16[8,128,896]{2,1,0:T(8,128)(2,1)S(1)}, u32[]{:S(2)}, u32[]{:S(2)}) async-start(bf16[8,128,896]{2,1,0:T(8,128)(2,1)} %get-tuple-element.11), calls=%async_computation.1 | async-start | bytes 3670016 | tf_op jit(solution)/shard_map/all_to_all | solution.py:209
  72.4 12.9 %all-gather.2.cloned.1.call-done = bf16[8192,128]{1,0:T(8,128)(2,1)} async-done(((bf16[1024,128]{1,0:T(8,128)(2,1)}), bf16[8192,128]{1,0:T(8,128)(2,1)}) %all-gather.2.cloned.1.call-update) | async-done | bytes 2097168 | tf_op jit(solution)/shard_map/all_gather | solution.py:175
  85.2 33.1 %all-to-all-done.1.rows_ref = bf16[8,128,896]{2,1,0:T(8,128)(2,1)S(1)} async-done(((bf16[8,128,896]{2,1,0:T(8,128)(2,1)}), bf16[8,128,896]{2,1,0:T(8,128)(2,1)S(1)}, u32[]{:S(2)}, u32[]{:S(2)}) %all-to-all-start.1) | async-done | bytes 1835040 | tf_op jit(solution)/shard_map/all_to_all | solution.py:209
  118.4 6.0 %shard_map.78 = (bf16[8,1024,128]{2,1,0:T(8,128)(2,1)}, f32[8,1,128]{2,1,0:T(1,128)S(1)}) custom-call(bf16[8,128,896]{2,1,0:T(8,128)(2,1)S(1)} %all-to-all-done.1.rows_ref, bf16[1,1024,896]{2,1,0:T(8,128)(2,1)} %weight_ref.1, bf16[8,1024,128]{2,1,0:T(8,128)(2,1)} %bitcast.48), custom_call_target="tpu_custom_call" | custom-call | flops 1879048192 | bytes 8000000 | tf_op jit(solution)/shard_map/pallas_call | solution.py:101
  124.4 0.7 copy-done
  125.6 3.3 %all-to-all-start.2 = ((f32[8,2,128]{2,1,0:T(2,128)}), f32[8,2,128]{2,1,0:T(2,128)S(1)}, u32[]{:S(2)}, u32[]{:S(2)}) async-start(f32[8,2,128]{2,1,0:T(2,128)} %pad_maximum_fusion.1), calls=%async_computation.3 | async-start | bytes 16384 | tf_op jit(solution)/shard_map/all_to_all | solution.py:217
  129.1 6.4 %all-to-all-done.2 = f32[8,2,128]{2,1,0:T(2,128)S(1)} async-done(((f32[8,2,128]{2,1,0:T(2,128)}), f32[8,2,128]{2,1,0:T(2,128)S(1)}, u32[]{:S(2)}, u32[]{:S(2)}) %all-to-all-start.2) | async-done | bytes 8224 | tf_op jit(solution)/shard_map/all_to_all | solution.py:217
  136.1 0.6 select_reduce_fusion
  136.8 0.8 copy.39
  137.6 7.7 %all-to-all-start.3 = ((f32[128,2,8]{2,1,0:T(2,128)}), f32[128,2,8]{2,1,0:T(2,128)S(1)}, u32[]{:S(2)}, u32[]{:S(2)}) async-start(f32[128,2,8]{2,1,0:T(2,128)} %bitcast.18), calls=%async_computation.4 | async-start | bytes 262144 | tf_op jit(solution)/shard_map/all_to_all | solution.py:226
  145.4 13.7 %all-to-all-done.3 = f32[128,2,8]{2,1,0:T(2,128)S(1)} async-done(((f32[128,2,8]{2,1,0:T(2,128)}), f32[128,2,8]{2,1,0:T(2,128)S(1)}, u32[]{:S(2)}, u32[]{:S(2)}) %all-to-all-start.3) | async-done | bytes 8224 | tf_op jit(solution)/shard_map/all_to_all | solution.py:226
  159.3 0.7 multiply_reduce_fusion
  159.9 2.3 %shard_map.79 = bf16[1,2,1024,128]{3,2,1,0:T(8,128)(2,1)} custom-call(bf16[1024,128]{1,0:T(8,128)(2,1)} %reduce-scatter.2.cloned.1.call-done.u_ref, bf16[1,1024,128]{2,1,0:T(8,128)(2,1)} %gate_ref.1, bf16[1,1024,128]{2,1,0:T(8,128)(2,1)} %up_ref.1, f32[8,1,128]{2,1,0:T(1,128)} %get-tuple-element.17.weight_ref), custom_call_target="tpu_custom_call" | custom-call | flops 3932160 | bytes 2000000 | tf_op jit(solution)/shard_map/pallas_call | solution.py:141
  (34 shorter events, 3.4 us)
Async XLA Ops:
  13.4 38.9 %all-to-all-start = ((bf16[128,16,128]{2,1,0:T(8,128)(2,1)}), bf16[128,16,128]{2,1,0:T(8,128)(2,1)S(1)}, u32[]{:S(2)}, u32[]{:S(2)}) async-start(bf16[128,16,128]{2,1,0:T(8,128)(2,1)} %bitcast.8), calls=%async_computation | async-start | bytes 1048576 | tf_op jit(solution)/shard_map/all_to_all | solution.py:192
  32.7 52.5 %all-gather.2.cloned.1.call-start = ((), (), s32[]{:S(2)}) async-start(), calls=%async_computation.5 | async-start | bytes 2359296 | tf_op jit(solution)/shard_map/all_gather | solution.py:175
  60.0 58.3 %all-to-all-start.1 = ((bf16[8,128,896]{2,1,0:T(8,128)(2,1)}), bf16[8,128,896]{2,1,0:T(8,128)(2,1)S(1)}, u32[]{:S(2)}, u32[]{:S(2)}) async-start(bf16[8,128,896]{2,1,0:T(8,128)(2,1)} %get-tuple-element.11), calls=%async_computation.1 | async-start | bytes 3670016 | tf_op jit(solution)/shard_map/all_to_all | solution.py:209
  72.3 87.6 %reduce-scatter.2.cloned.1.call-start = ((), (), s32[]{:S(2)}) async-start(), calls=%async_computation.6 | async-start | bytes 2359296 | tf_op jit(solution)/shard_map/reduce_scatter | solution.py:212
  124.3 0.7 copy-start
  125.6 9.9 %all-to-all-start.2 = ((f32[8,2,128]{2,1,0:T(2,128)}), f32[8,2,128]{2,1,0:T(2,128)S(1)}, u32[]{:S(2)}, u32[]{:S(2)}) async-start(f32[8,2,128]{2,1,0:T(2,128)} %pad_maximum_fusion.1), calls=%async_computation.3 | async-start | bytes 16384 | tf_op jit(solution)/shard_map/all_to_all | solution.py:217
  137.6 21.5 %all-to-all-start.3 = ((f32[128,2,8]{2,1,0:T(2,128)}), f32[128,2,8]{2,1,0:T(2,128)S(1)}, u32[]{:S(2)}, u32[]{:S(2)}) async-start(f32[128,2,8]{2,1,0:T(2,128)} %bitcast.18), calls=%async_computation.4 | async-start | bytes 262144 | tf_op jit(solution)/shard_map/all_to_all | solution.py:226
Sparse Core Ops, SparseCore 0:
  36.2 48.9 all-gather.1
  124.5 33.6 reduce-scatter.1

commit v3 on v2

--- a/solution.py
+++ b/solution.py
@@ -15,41 +15,34 @@
 
 
 def pick_kernel(lines_ref, rows_ref, out_ref, slot_weight_ref):
-    expert = pl.program_id(0)
-    experts = lines_ref.shape[0] // 2
-    lines = lines_ref[...]
-    line = lax.broadcasted_iota(jnp.int32, lines.shape, 0)
-    slot_of = jnp.sum(jnp.where(line == expert, lines, 0.0), axis=0, keepdims=True)
-    weight_of = jnp.sum(jnp.where(line == expert + experts, lines, 0.0), axis=0, keepdims=True)
-    _, slots, _ = out_ref.shape
-    slot = lax.broadcasted_iota(jnp.int32, (slots, lines.shape[1]), 0).astype(F32)
-    holds = jnp.where(slot_of == slot, 1.0, 0.0).astype(BF16)
-    out_ref[0] = jnp.dot(holds, rows_ref[...], preferred_element_type=F32).astype(BF16)
-    weights = jnp.broadcast_to(weight_of, (8, lines.shape[1])).astype(BF16)
-    slot_weight_ref[0] = lax.dot_general(
-        weights, holds, (((1,), (1,)), ((), ())), preferred_element_type=F32
-    )[:1]
+    experts, slots, _ = out_ref.shape
+    row_count = rows_ref.shape[0]
+    slot = lax.broadcasted_iota(jnp.int32, (slots, row_count), 0).astype(F32)
+    for expert in range(experts):
+        holds = jnp.where(lines_ref[expert : expert + 1, :] == slot, 1.0, 0.0).astype(BF16)
+        out_ref[expert] = jnp.dot(holds, rows_ref[...], preferred_element_type=F32).astype(BF16)
+        weights = lines_ref[experts + expert : experts + expert + 1, :].astype(BF16)
+        slot_weight_ref[expert] = lax.dot_general(
+            jnp.broadcast_to(weights, (8, row_count)),
+            holds,
+            (((1,), (1,)), ((), ())),
+            preferred_element_type=F32,
+        )[:1]
 
 
 def pick(lines, rows, slots):
     experts = lines.shape[0] // 2
     row_count, width = rows.shape
+    vmem = pl.BlockSpec(memory_space=pltpu.VMEM)
     return pl.pallas_call(
         pick_kernel,
-        grid=(experts,),
-        in_specs=[
-            pl.BlockSpec(lines.shape, lambda e: (0, 0)),
-            pl.BlockSpec(rows.shape, lambda e: (0, 0)),
-        ],
-        out_specs=[
-            pl.BlockSpec((1, slots, width), lambda e: (e, 0, 0)),
-            pl.BlockSpec((1, 1, slots), lambda e: (e, 0, 0)),
-        ],
+        in_specs=[vmem, vmem],
+        out_specs=[vmem, vmem],
         out_shape=[
             jax.ShapeDtypeStruct((experts, slots, width), BF16),
             jax.ShapeDtypeStruct((experts, 1, slots), F32),
         ],
-        compiler_params=pltpu.CompilerParams(vmem_limit_bytes=60 * 1024 * 1024),
+        compiler_params=pltpu.CompilerParams(vmem_limit_bytes=32 * 1024 * 1024),
         cost_estimate=pl.CostEstimate(
             flops=2 * experts * slots * row_count * width, bytes_accessed=2_500_000, transcendentals=0
         ),
@@ -72,54 +65,62 @@
     return jnp.sum(jnp.where(same, line, 0.0), axis=1, keepdims=True)
 
 
-def product_kernel(rows_ref, weight_ref, hidden_ref, out_ref, dot_ref, total):
-    step = pl.program_id(0)
+def product_kernel(rows_ref, weight_ref, out_ref):
     z_count, slots, width = rows_ref.shape
     rows = rows_ref[...].reshape(z_count * slots, width)
     term = lax.dot_general(
         rows, weight_ref[0], (((1,), (1,)), ((), ())), preferred_element_type=F32
     ).astype(BF16)
-    dots = jnp.where(step == 0, 0.0, total[...])
     for block in range(out_ref.shape[0]):
-        part = term[:, block * LANES : (block + 1) * LANES]
-        out_ref[block] = part
-        dots += part.astype(F32) * hidden_ref[block].astype(F32)
-    total[...] = dots
-
-    @pl.when(step == pl.num_programs(0) - 1)
-    def _():
-        for z in range(z_count):
-            summed = jnp.sum(total[z * slots : (z + 1) * slots, :], axis=1, keepdims=True)
-            dot_ref[z] = as_line(summed)
-
-
-def product(rows, weight, hidden):
+        out_ref[block] = term[:, block * LANES : (block + 1) * LANES]
+
+
+def product(rows, weight):
     z_count, slots, width = rows.shape
-    blocks, slot_count, lanes = hidden.shape
     units = weight.shape[1]
+    slot_count = z_count * slots
     per_step = 2
     return pl.pallas_call(
         product_kernel,
-        grid=(blocks // per_step,),
+        grid=(units // LANES // per_step,),
         in_specs=[
             pl.BlockSpec((z_count, slots, width), lambda i: (0, 0, 0)),
-            pl.BlockSpec((1, per_step * lanes, width), lambda i: (0, i, 0)),
-            pl.BlockSpec((per_step, slot_count, lanes), lambda i: (i, 0, 0)),
+            pl.BlockSpec((1, per_step * LANES, width), lambda i: (0, i, 0)),
         ],
-        out_specs=[
-            pl.BlockSpec((per_step, slot_count, lanes), lambda i: (i, 0, 0)),
-            pl.BlockSpec((z_count, 1, slots), lambda i: (0, 0, 0)),
-        ],
-        out_shape=[
-            jax.ShapeDtypeStruct((blocks, slot_count, lanes), BF16),
-            jax.ShapeDtypeStruct((z_count, 1, slots), F32),
-        ],
-        scratch_shapes=[pltpu.VMEM((slot_count, lanes), F32)],
+        out_specs=pl.BlockSpec((per_step, slot_count, LANES), lambda i: (i, 0, 0)),
+        out_shape=jax.ShapeDtypeStruct((units // LANES, slot_count, LANES), BF16),
         compiler_params=pltpu.CompilerParams(vmem_limit_bytes=52 * 1024 * 1024),
         cost_estimate=pl.CostEstimate(
-            flops=2 * slot_count * width * units, bytes_accessed=8_000_000, transcendentals=0
-        ),
-    )(rows, weight, hidden)
+            flops=2 * slot_count * width * units, bytes_accessed=6_000_000, transcendentals=0
+        ),
+    )(rows, weight)
+
+
+def dots_kernel(term_ref, hidden_ref, dot_ref):
+    z_count, _, slots = dot_ref.shape
+    total = term_ref[0].astype(F32) * hidden_ref[0].astype(F32)
+    for block in range(1, term_ref.shape[0]):
+        total += term_ref[block].astype(F32) * hidden_ref[block].astype(F32)
+    for z in range(z_count):
+        dot_ref[z] = as_line(jnp.sum(total[z * slots : (z + 1) * slots, :], axis=1, keepdims=True))
+
+
+def dots_of(term, hidden, z_count):
+    blocks, slot_count, lanes = hidden.shape
+    slots = slot_count // z_count
+    per_step = z_count // 4
+    block = pl.BlockSpec((blocks, per_step * slots, lanes), lambda i: (0, i, 0))
+    return pl.pallas_call(
+        dots_kernel,
+        grid=(4,),
+        in_specs=[block, block],
+        out_specs=pl.BlockSpec((per_step, 1, slots), lambda i: (i, 0, 0)),
+        out_shape=jax.ShapeDtypeStruct((z_count, 1, slots), F32),
+        compiler_params=pltpu.CompilerParams(vmem_limit_bytes=60 * 1024 * 1024),
+        cost_estimate=pl.CostEstimate(
+            flops=2 * blocks * slot_count * lanes, bytes_accessed=4_000_000, transcendentals=0
+        ),
+    )(term, hidden)
 
 
 def gate_kernel(u_ref, gate_ref, up_ref, weight_ref, grad_ref):
@@ -171,7 +172,6 @@
 
     a = gate_pre[0].astype(F32)
     hidden = (a * (1.0 / (1.0 + jnp.exp(-a))) * up_pre[0].astype(F32)).astype(BF16)
-    hidden, expert_ids, route_weights = lax.optimization_barrier((hidden, expert_ids, route_weights))
     hidden_all = lax.all_gather(hidden, "x", tiled=True).reshape(n_x, hidden.shape[0], LANES)
 
     group_iota = jnp.arange(n_node, dtype=jnp.int32)
@@ -208,7 +208,8 @@
     picked, slot_weight = pick(lines, rows, slots)
     taken = lax.all_to_all(picked, "z", split_axis=0, concat_axis=0, tiled=True)
 
-    partial, dots = product(taken, down_weight, hidden_all)
+    partial = product(taken, down_weight)
+    dots = dots_of(partial, hidden_all, n_z)
     u = lax.psum_scatter(
         partial.reshape(n_x * n_z * slots, LANES), "x", scatter_dimension=0, tiled=True
     )

time: 171 us -> 165 us (0.965)
  blocking collectives: 0 us -> 56 us
  waiting for transfers between devices: 85.5 us -> 38.4 us
  starting transfers between devices: 42.8 us -> 32.7 us
    all_to_all x0 -> x1, blocking collectives: none -> 56 us  [body(): taken = lax.all_to_all(picked, 'z', split_axis=0, concat_axis=0, tiled=True)]
    all_to_all x1 -> x0, waiting for transfers between devices: 33.1 us -> none  [body(): taken = lax.all_to_all(picked, 'z', split_axis=0, concat_axis=0, tiled=True)]
    all_gather x1, waiting for transfers between devices: 12.9 us -> 0.02 us  [body(): lax.all_gather(hidden, 'x', tiled=True).reshape(n_x, hidden.shape[0], LANES)]
    all_to_all x1 -> x0, starting transfers between devices: 12.3 us -> none  [body(): taken = lax.all_to_all(picked, 'z', split_axis=0, concat_axis=0, tiled=True)]
    all_to_all x1, starting transfers between devices: 7.75 us -> 9.88 us  [body(): lax.all_to_all(value, ('node', 'x'), split_axis=0, concat_axis=0, tiled=T...]
    pallas_call x2 -> x3, Pallas kernels: 11 us -> 10.2 us  [the longest x1 5.35 us: product(): pl.pallas_call(product_kernel, grid=(units // LANES // per_step,), in_spe...]
  transfers between devices with their start and end apart: 6 -> 5, of which waited for: 5 -> 3; matrix products, arithmetic and copies ran while one was open for 4% -> 4% of each run, Pallas kernels for 3% -> 6%
where the time goes in v3:
time: 165 us
  blocking collectives  56 us (34%)
  waiting for transfers between devices  38.4 us (23%)
  starting transfers between devices  32.7 us (20%)
  between operations  14.3 us (9%)
  Pallas kernels  12.6 us (8%)
  other arithmetic  5.79 us (4%)
  local copies, waits for them, and re-layouts  3.66 us (2%)
    all_to_all x1, blocking collectives, body(): taken = lax.all_to_all(picked, 'z', split_axis=0, concat_axis=0, tiled=True)  56 us
    all_to_all x1, starting transfers between devices, body(): lax.all_to_all(send, ('node', 'x'), split_axis=0, concat_axis=0, tiled=True)  19.4 us
    all_to_all x1, waiting for transfers between devices, body(): lax.all_to_all(send, ('node', 'x'), split_axis=0, concat_axis=0, tiled=True)  18.5 us
    all_to_all x1, waiting for transfers between devices, body(): lax.all_to_all(value, ('node', 'x'), split_axis=0, concat_axis=0, tiled=T...  13.5 us
    all_to_all x1, starting transfers between devices, body(): lax.all_to_all(value, ('node', 'x'), split_axis=0, concat_axis=0, tiled=T...  9.88 us
    all_to_all x1, waiting for transfers between devices, body(): both = lax.all_to_all(both, 'z', split_axis=0, concat_axis=0, tiled=True)  6.38 us
    pallas_call x1, Pallas kernels, product(): pl.pallas_call(product_kernel, grid=(units // LANES // per_step,), in_spe...  5.35 us
    pallas_call x1, Pallas kernels, dots_of(): pl.pallas_call(dots_kernel, grid=(4,), in_specs=[block, block], out_specs...  4.02 us
  transfers between devices with their start and end apart: 5, of which 3 were waited for; matrix products, arithmetic and copies ran while one was open for 4% of the time, Pallas kernels for 6%

profile of v3, /device:TPU:1, one launch (start us, length us, event | category | flops | bytes accessed | tf_op | source)
XLA Modules:
  0.0 164.8 jit_solution(18372526871812614242)
XLA Ops:
  7.2 0.8 add_select_fusion
  8.1 0.8 fusion.27
  8.8 1.2 convolution_convert_fusion
  10.6 0.9 copy.32
  11.5 19.4 %all-to-all-start = ((bf16[128,16,128]{2,1,0:T(8,128)(2,1)}), bf16[128,16,128]{2,1,0:T(8,128)(2,1)S(1)}, u32[]{:S(2)}, u32[]{:S(2)}) async-start(bf16[128,16,128]{2,1,0:T(8,128)(2,1)} %bitcast.5), calls=%async_computation | async-start | bytes 1048576 | tf_op jit(solution)/shard_map/all_to_all | solution.py:192
  30.9 0.9 fusion.5
  31.9 18.5 %all-to-all-done = bf16[128,16,128]{2,1,0:T(8,128)(2,1)S(1)} async-done(((bf16[128,16,128]{2,1,0:T(8,128)(2,1)}), bf16[128,16,128]{2,1,0:T(8,128)(2,1)S(1)}, u32[]{:S(2)}, u32[]{:S(2)}) %all-to-all-start) | async-done | bytes 524320 | tf_op jit(solution)/shard_map/all_to_all | solution.py:192
  50.9 0.2 fusion
  51.2 0.3 copy.35
  51.6 0.2 copy.36.rows_ref
  51.9 0.9 shard_map.77
  52.7 56.0 %all_to_all.20.rows_ref = bf16[8,128,896]{2,1,0:T(8,128)(2,1)S(1)} all-to-all(bf16[8,128,896]{2,1,0:T(8,128)(2,1)S(1)} %get-tuple-element.4), channel_id=1, replica_groups=mesh['node'=16,'z'=8,'x'=8] {'z'}, dimensions={0} | all-to-all | bytes 3670016 | tf_op jit(solution)/shard_map/all_to_all | solution.py:209
  108.7 5.3 %shard_map.78.term_ref = bf16[8,1024,128]{2,1,0:T(8,128)(2,1)} custom-call(bf16[8,128,896]{2,1,0:T(8,128)(2,1)S(1)} %all_to_all.20.rows_ref, bf16[1,1024,896]{2,1,0:T(8,128)(2,1)} %weight_ref.1), custom_call_target="tpu_custom_call" | custom-call | flops 1879048192 | bytes 6000000 | tf_op jit(solution)/shard_map/pallas_call | solution.py:83
  114.1 4.0 %shard_map.79 = f32[8,1,128]{2,1,0:T(1,128)} custom-call(bf16[8,1024,128]{2,1,0:T(8,128)(2,1)} %shard_map.78.term_ref, bf16[8,1024,128]{2,1,0:T(8,128)(2,1)} %bitcast.40), custom_call_target="tpu_custom_call" | custom-call | flops 2097152 | bytes 4000000 | tf_op jit(solution)/shard_map/pallas_call | solution.py:113
  118.1 1.3 pad_maximum_fusion.1
  119.4 3.3 %all-to-all-start.2 = ((f32[8,2,128]{2,1,0:T(2,128)}), f32[8,2,128]{2,1,0:T(2,128)S(1)}, u32[]{:S(2)}, u32[]{:S(2)}) async-start(f32[8,2,128]{2,1,0:T(2,128)} %pad_maximum_fusion.1), calls=%async_computation.3 | async-start | bytes 16384 | tf_op jit(solution)/shard_map/all_to_all | solution.py:218
  122.9 6.4 %all-to-all-done.2 = f32[8,2,128]{2,1,0:T(2,128)S(1)} async-done(((f32[8,2,128]{2,1,0:T(2,128)}), f32[8,2,128]{2,1,0:T(2,128)S(1)}, u32[]{:S(2)}, u32[]{:S(2)}) %all-to-all-start.2) | async-done | bytes 8224 | tf_op jit(solution)/shard_map/all_to_all | solution.py:218
  129.3 0.6 fusion.30
  129.9 0.6 select_reduce_fusion
  130.6 0.8 copy.39
  131.4 9.9 %all-to-all-start.3 = ((f32[128,2,8]{2,1,0:T(2,128)}), f32[128,2,8]{2,1,0:T(2,128)S(1)}, u32[]{:S(2)}, u32[]{:S(2)}) async-start(f32[128,2,8]{2,1,0:T(2,128)} %bitcast.18), calls=%async_computation.4 | async-start | bytes 262144 | tf_op jit(solution)/shard_map/all_to_all | solution.py:227
  141.3 13.5 %all-to-all-done.3 = f32[128,2,8]{2,1,0:T(2,128)S(1)} async-done(((f32[128,2,8]{2,1,0:T(2,128)}), f32[128,2,8]{2,1,0:T(2,128)S(1)}, u32[]{:S(2)}, u32[]{:S(2)}) %all-to-all-start.3) | async-done | bytes 8224 | tf_op jit(solution)/shard_map/all_to_all | solution.py:227
  154.9 0.7 multiply_reduce_fusion
  155.6 2.3 %shard_map.80 = bf16[1,2,1024,128]{3,2,1,0:T(8,128)(2,1)} custom-call(bf16[1024,128]{1,0:T(8,128)(2,1)} %reduce-scatter.2.cloned.1.call-done.u_ref, bf16[1,1024,128]{2,1,0:T(8,128)(2,1)} %gate_ref.1, bf16[1,1024,128]{2,1,0:T(8,128)(2,1)} %up_ref.1, f32[8,1,128]{2,1,0:T(1,128)} %get-tuple-element.7.weight_ref), custom_call_target="tpu_custom_call" | custom-call | flops 3932160 | bytes 2000000 | tf_op jit(solution)/shard_map/pallas_call | solution.py:142
  (36 shorter events, 1.7 us)
Async XLA Ops:
  10.4 20.5 %copy-start = (bf16[1,1024,128]{2,1,0:T(8,128)(2,1)S(1)}, bf16[1,1024,128]{2,1,0:T(8,128)(2,1)}, u32[]{:S(2)}) copy-start(bf16[1,1024,128]{2,1,0:T(8,128)(2,1)} %up_ref.1) | copy-start | bytes 786436
  10.5 20.5 %copy-start.1 = (bf16[1,1024,128]{2,1,0:T(8,128)(2,1)S(1)}, bf16[1,1024,128]{2,1,0:T(8,128)(2,1)}, u32[]{:S(2)}) copy-start(bf16[1,1024,128]{2,1,0:T(8,128)(2,1)} %gate_ref.1) | copy-start | bytes 786436
  11.5 38.9 %all-to-all-start = ((bf16[128,16,128]{2,1,0:T(8,128)(2,1)}), bf16[128,16,128]{2,1,0:T(8,128)(2,1)S(1)}, u32[]{:S(2)}, u32[]{:S(2)}) async-start(bf16[128,16,128]{2,1,0:T(8,128)(2,1)} %bitcast.5), calls=%async_computation | async-start | bytes 1048576 | tf_op jit(solution)/shard_map/all_to_all | solution.py:192
  30.9 83.2 %all-gather.2.cloned.1.call-start = ((), (), s32[]{:S(2)}) async-start(), calls=%async_computation.6 | async-start | bytes 2359296 | tf_op jit(solution)/shard_map/all_gather | solution.py:175
  31.8 123.8 %reduce-scatter.2.cloned.1.call-start = ((), (), s32[]{:S(2)}) async-start(), calls=%async_computation.5 | async-start | bytes 2359296 | tf_op jit(solution)/shard_map/reduce_scatter | solution.py:213
  119.4 9.9 %all-to-all-start.2 = ((f32[8,2,128]{2,1,0:T(2,128)}), f32[8,2,128]{2,1,0:T(2,128)S(1)}, u32[]{:S(2)}, u32[]{:S(2)}) async-start(f32[8,2,128]{2,1,0:T(2,128)} %pad_maximum_fusion.1), calls=%async_computation.3 | async-start | bytes 16384 | tf_op jit(solution)/shard_map/all_to_all | solution.py:218
  131.4 23.4 %all-to-all-start.3 = ((f32[128,2,8]{2,1,0:T(2,128)}), f32[128,2,8]{2,1,0:T(2,128)S(1)}, u32[]{:S(2)}, u32[]{:S(2)}) async-start(f32[128,2,8]{2,1,0:T(2,128)} %bitcast.18), calls=%async_computation.4 | async-start | bytes 262144 | tf_op jit(solution)/shard_map/all_to_all | solution.py:227
Sparse Core Ops, SparseCore 0:
  34.4 48.9 all-gather.1
  114.2 36.0 reduce-scatter.1

commit v4 on v3

v4 whole, which is shorter than its diff:
```python
import functools

import jax
import jax.numpy as jnp
from jax import lax
from jax.experimental import pallas as pl
from jax.experimental.pallas import tpu as pltpu
from jax.sharding import Mesh
from jax.sharding import PartitionSpec as P

EPG = 8
LANES = 128
F32 = jnp.float32
BF16 = jnp.bfloat16


def iota(shape, axis):
    return lax.broadcasted_iota(jnp.int32, shape, axis)


def one_where(mask):
    return jnp.where(mask, 1.0, 0.0)


def send_kernel(grad_ref, ids_ref, weights_ref, out_ref, chosen_ref, *, experts):
    nodes, slices, lines, _ = out_ref.shape
    tokens, top_count = ids_ref.shape
    tiles = grad_ref.shape[1] // slices // LANES
    parts = tiles + 1
    per_group = lines // parts
    ids = ids_ref[...].astype(F32)
    columns = parts * tokens
    spread = one_where(iota((tokens, columns), 0) == iota((tokens, columns), 1) % tokens)
    named = lax.dot_general(ids, spread, (((0,), (0,)), ((), ())), preferred_element_type=F32)
    named_group = named.astype(jnp.int32) // experts
    shape = (nodes * lines, columns)
    line, column = iota(shape, 0), iota(shape, 1)
    group, rank, part = line // lines, line // parts % per_group, line % parts
    reaches = jnp.zeros(shape, F32)
    for place in range(top_count):
        reaches = jnp.where(named_group[place : place + 1, :] == group, 1.0, reaches)
    square = (columns, columns)
    before = one_where((iota(square, 0) < tokens) & (iota(square, 0) < iota(square, 1) % tokens))
    order = jnp.dot(reaches, before, preferred_element_type=F32)
    chosen = jnp.where(
        (order == rank.astype(F32)) & (part == column // tokens), reaches, 0.0
    ).astype(BF16)
    picks = (chosen_ref.shape[0], nodes * lines)
    first_lines = one_where(iota(picks, 0) * parts == iota(picks, 1)).astype(BF16)
    chosen_ref[...] = jnp.dot(first_lines, chosen, preferred_element_type=F32)[:, :tokens]
    place = (top_count, LANES)
    tail = jnp.dot(ids, one_where(iota(place, 0) == iota(place, 1)), preferred_element_type=F32)
    tail += jnp.dot(
        weights_ref[...].astype(F32),
        one_where(iota(place, 0) + top_count == iota(place, 1)),
        preferred_element_type=F32,
    )
    for piece in range(slices):
        first = piece * tiles
        source = [
            grad_ref[:, (first + tile) * LANES : (first + tile + 1) * LANES].astype(F32) for tile in range(tiles)
        ]
        source = jnp.concatenate(source + [tail], axis=0).astype(BF16)
        rows = jnp.dot(chosen, source, preferred_element_type=F32).astype(BF16)
        out_ref[:, piece] = rows.reshape(nodes, lines, LANES)


def send_rows(out_grad, expert_ids, route_weights, nodes, slices, experts, per_group):
    lines = per_group * (out_grad.shape[1] // slices // LANES + 1)
    return pl.pallas_call(
        functools.partial(send_kernel, experts=experts),
        out_shape=[
            jax.ShapeDtypeStruct((nodes, slices, lines, LANES), BF16),
            jax.ShapeDtypeStruct((nodes * per_group, out_grad.shape[0]), F32),
        ],
        compiler_params=pltpu.CompilerParams(vmem_limit_bytes=32 * 1024 * 1024),
        cost_estimate=pl.CostEstimate(flops=40_000_000, bytes_accessed=700_000, transcendentals=0),
    )(out_grad, expert_ids, route_weights)


def pick_kernel(lines_ref, rows_ref, first_ref, second_ref, slot_weight_ref):
    experts, half, _ = first_ref.shape
    slots = 2 * half
    row_count = rows_ref.shape[0]
    slot = lax.broadcasted_iota(jnp.int32, (slots, row_count), 0).astype(F32)
    for expert in range(experts):
        holds = jnp.where(lines_ref[expert : expert + 1, :] == slot, 1.0, 0.0).astype(BF16)
        first_ref[expert] = jnp.dot(
            holds[:half], rows_ref[...], preferred_element_type=F32
        ).astype(BF16)
        second_ref[expert] = jnp.dot(
            holds[half:], rows_ref[...], preferred_element_type=F32
        ).astype(BF16)
        weights = lines_ref[experts + expert : experts + expert + 1, :].astype(BF16)
        slot_weight_ref[expert] = lax.dot_general(
            jnp.broadcast_to(weights, (8, row_count)),
            holds,
            (((1,), (1,)), ((), ())),
            preferred_element_type=F32,
        )[:1]


def pick(lines, rows, slots):
    experts = lines.shape[0] // 2
    row_count, width = rows.shape
    vmem = pl.BlockSpec(memory_space=pltpu.VMEM)
    return pl.pallas_call(
        pick_kernel,
        in_specs=[vmem, vmem],
        out_specs=[vmem, vmem, vmem],
        out_shape=[
            jax.ShapeDtypeStruct((experts, slots // 2, width), BF16),
            jax.ShapeDtypeStruct((experts, slots // 2, width), BF16),
            jax.ShapeDtypeStruct((experts, 1, slots), F32),
        ],
        compiler_params=pltpu.CompilerParams(vmem_limit_bytes=32 * 1024 * 1024),
        cost_estimate=pl.CostEstimate(
            flops=2 * experts * slots * row_count * width, bytes_accessed=2_500_000, transcendentals=0
        ),
    )(lines, rows)


def as_line(column):
    count = column.shape[0]
    same = lax.broadcasted_iota(jnp.int32, (count, count), 0) == lax.broadcasted_iota(
        jnp.int32, (count, count), 1
    )
    return jnp.sum(jnp.where(same, column, 0.0), axis=0, keepdims=True)


def as_column(line):
    count = line.shape[1]
    same = lax.broadcasted_iota(jnp.int32, (count, count), 0) == lax.broadcasted_iota(
        jnp.int32, (count, count), 1
    )
    return jnp.sum(jnp.where(same, line, 0.0), axis=1, keepdims=True)


def product_kernel(first_ref, second_ref, weight_ref, out_ref):
    z_count, half, width = first_ref.shape
    for part, rows_ref in enumerate((first_ref, second_ref)):
        rows = rows_ref[...].reshape(z_count * half, width)
        term = lax.dot_general(
            rows, weight_ref[0], (((1,), (1,)), ((), ())), preferred_element_type=F32
        ).astype(BF16)
        for block in range(out_ref.shape[0]):
            lanes = term[:, block * LANES : (block + 1) * LANES]
            out_ref[block, :, part] = lanes.reshape(z_count, half, LANES)


def product(first, second, weight):
    z_count, half, width = first.shape
    units = weight.shape[1]
    per_step = 2
    rows = pl.BlockSpec((z_count, half, width), lambda i: (0, 0, 0))
    return pl.pallas_call(
        product_kernel,
        grid=(units // LANES // per_step,),
        in_specs=[rows, rows, pl.BlockSpec((1, per_step * LANES, width), lambda i: (0, i, 0))],
        out_specs=pl.BlockSpec((per_step, z_count, 2, half, LANES), lambda i: (i, 0, 0, 0, 0)),
        out_shape=jax.ShapeDtypeStruct((units // LANES, z_count, 2, half, LANES), BF16),
        compiler_params=pltpu.CompilerParams(vmem_limit_bytes=52 * 1024 * 1024),
        cost_estimate=pl.CostEstimate(
            flops=4 * z_count * half * width * units, bytes_accessed=6_000_000, transcendentals=0
        ),
    )(first, second, weight)


def dots_kernel(term_ref, hidden_ref, weight_ref, both_ref):
    z_count, _, slots = both_ref.shape
    total = term_ref[0].astype(F32) * hidden_ref[0].astype(F32)
    for block in range(1, term_ref.shape[0]):
        total += term_ref[block].astype(F32) * hidden_ref[block].astype(F32)
    for z in range(z_count):
        both_ref[z, 0:1] = as_line(jnp.sum(total[z * slots : (z + 1) * slots, :], axis=1, keepdims=True))
        both_ref[z, 1:2] = weight_ref[z]


def dots_of(term, hidden, slot_weight):
    blocks, slot_count, lanes = hidden.shape
    z_count, _, slots = slot_weight.shape
    per_step = z_count // 4
    block = pl.BlockSpec((blocks, per_step * slots, lanes), lambda i: (0, i, 0))
    return pl.pallas_call(
        dots_kernel,
        grid=(4,),
        in_specs=[block, block, pl.BlockSpec((per_step, 1, slots), lambda i: (i, 0, 0))],
        out_specs=pl.BlockSpec((per_step, 2, slots), lambda i: (i, 0, 0)),
        out_shape=jax.ShapeDtypeStruct((z_count, 2, slots), F32),
        compiler_params=pltpu.CompilerParams(vmem_limit_bytes=60 * 1024 * 1024),
        cost_estimate=pl.CostEstimate(
            flops=2 * blocks * slot_count * lanes, bytes_accessed=4_000_000, transcendentals=0
        ),
    )(term, hidden, slot_weight)


def gate_kernel(u_ref, gate_ref, up_ref, weight_ref, grad_ref):
    u = u_ref[...].astype(F32)
    a = gate_ref[0].astype(F32)
    b = up_ref[0].astype(F32)
    s = 1.0 / (1.0 + jnp.exp(-a))
    weight = jnp.concatenate([as_column(weight_ref[z, 1:2]) for z in range(weight_ref.shape[0])], axis=0)
    scaled = weight * u
    grad_ref[0, 0] = (scaled * b * s * (1.0 + a * (1.0 - s))).astype(BF16)
    grad_ref[0, 1] = (scaled * a * s).astype(BF16)


def gate(u, gate_pre, up_pre, both):
    z_count, _, slots = both.shape
    slot_count, width = u.shape
    per_step = z_count // 2
    lines = per_step * slots
    return pl.pallas_call(
        gate_kernel,
        grid=(2,),
        in_specs=[
            pl.BlockSpec((lines, width), lambda z: (z, 0)),
            pl.BlockSpec((1, lines, width), lambda z: (0, z, 0)),
            pl.BlockSpec((1, lines, width), lambda z: (0, z, 0)),
            pl.BlockSpec((per_step, 2, slots), lambda z: (z, 0, 0)),
        ],
        out_specs=pl.BlockSpec((1, 2, lines, width), lambda z: (0, 0, z, 0)),
        out_shape=jax.ShapeDtypeStruct((1, 2, slot_count, width), BF16),
        compiler_params=pltpu.CompilerParams(vmem_limit_bytes=60 * 1024 * 1024),
        cost_estimate=pl.CostEstimate(
            flops=30 * slot_count * width, bytes_accessed=2_000_000, transcendentals=slot_count * width
        ),
    )(u, gate_pre, up_pre, both)


def body(out_grad, expert_ids, route_weights, down_weight, gate_pre, up_pre):
    n_node = lax.axis_size("node")
    n_z = lax.axis_size("z")
    n_x = lax.axis_size("x")
    tok_dev, model_width = out_grad.shape
    top_count = expert_ids.shape[1]
    width = model_width // n_x
    cap_group = 4 * tok_dev // n_node
    cap_expert = 2 * tok_dev
    slots = n_x * cap_expert
    row_count = n_node * n_x * cap_group
    tiles = width // LANES

    a = gate_pre[0].astype(F32)
    hidden = (a * (1.0 / (1.0 + jnp.exp(-a))) * up_pre[0].astype(F32)).astype(BF16)
    hidden_all = lax.all_gather(hidden, "x", tiled=True).reshape(n_x, hidden.shape[0], LANES)

    send, chosen = send_rows(out_grad, expert_ids, route_weights, n_node, n_x, n_z, cap_group)
    send = send.reshape(n_node * n_x, cap_group * (tiles + 1), LANES)
    got = lax.all_to_all(send, ("node", "x"), split_axis=0, concat_axis=0, tiled=True)
    got = got.reshape(row_count, tiles + 1, LANES)

    rows = got[:, :tiles].reshape(row_count, width)
    ids = got[:, tiles, :top_count].astype(F32).astype(jnp.int32)
    weights = got[:, tiles, top_count : 2 * top_count].astype(F32)
    my_group = lax.axis_index("node")
    member = (ids - my_group * n_z)[:, None, :] == jnp.arange(n_z, dtype=jnp.int32)[None, :, None]
    named_by = jnp.any(member, axis=2)
    weight_each = jnp.sum(jnp.where(member, weights[:, None, :], 0.0), axis=2)
    row = jnp.arange(row_count, dtype=jnp.int32)
    relay = row // cap_group % n_x
    earlier = (row[None, :] < row[:, None]) & (relay[None, :] == relay[:, None])
    place = jnp.dot(earlier.astype(BF16), named_by.astype(BF16), preferred_element_type=F32)
    slot_each = jnp.where(named_by, (relay * cap_expert).astype(F32)[:, None] + place, -1.0)
    lines = jnp.concatenate([slot_each.T, weight_each.T], axis=0)
    first, second, slot_weight = pick(lines, rows, slots)
    first = lax.all_to_all(first, "z", split_axis=0, concat_axis=0, tiled=True)
    second = lax.all_to_all(second, "z", split_axis=0, concat_axis=0, tiled=True)

    partial = product(first, second, down_weight).reshape(n_x, n_z * slots, LANES)
    u = lax.psum_scatter(
        partial.reshape(n_x * n_z * slots, LANES), "x", scatter_dimension=0, tiled=True
    )

    both = dots_of(partial, hidden_all, slot_weight)
    both = lax.all_to_all(both, "z", split_axis=0, concat_axis=0, tiled=True)
    dots = both[:, 0]
    grad_pre = gate(u, gate_pre, up_pre, both)
    slot_iota = jnp.arange(slots, dtype=jnp.int32).astype(F32)
    value = jnp.sum(
        jnp.where(slot_each[:, :, None] == slot_iota, dots[None], 0.0), axis=2
    )
    value = jnp.sum(jnp.where(member, value[:, :, None], 0.0), axis=1)
    value = value.reshape(n_node * n_x, cap_group, top_count)
    back = lax.all_to_all(value, ("node", "x"), split_axis=0, concat_axis=0, tiled=True)
    back = jnp.sum(back.reshape(n_node, n_x, cap_group, top_count), axis=1)
    chosen = chosen.reshape(n_node, cap_group, tok_dev)
    grad_weights = jnp.sum(chosen[..., None] * back[:, :, None, :], axis=(0, 1))
    return (grad_pre, grad_weights)


def solution(mesh):
    devices = mesh.devices
    n_node, n_local = devices.shape
    split = Mesh(devices.reshape(n_node, EPG, n_local // EPG), ("node", "z", "x"))
    first = ("node", "z", "x")
    return jax.shard_map(
        body,
        mesh=split,
        in_specs=(
            P(first, None),
            P(first, None),
            P(first, None),
            P(first, None, None),
            P(first, None, None),
            P(first, None, None),
        ),
        out_specs=(P(first, None, None, None), P(first, None)),
        check_vma=False,
    )
```

time: 165 us -> 173 us (1.048)
  blocking collectives: 56 us -> 62.1 us
  starting transfers between devices: 32.7 us -> 35.3 us
  Pallas kernels: 12.6 us -> 14.7 us
  other arithmetic: 5.79 us -> 3.8 us
    all_to_all x1 -> x2, blocking collectives: 56 us -> 62.1 us  [the longest x1 36.8 us: body(): first = lax.all_to_all(first, 'z', split_axis=0, concat_axis=0, tiled=True)]
    all_to_all x1, starting transfers between devices: 9.88 us -> 12.5 us  [body(): lax.all_to_all(value, ('node', 'x'), split_axis=0, concat_axis=0, tiled=T...]
    unnamed x6 -> x11, local copies, waits for them, and re-layouts: 0.09 us -> 2.34 us
    pallas_call x2 -> x3, Pallas kernels: 4.9 us -> 7.04 us  [the longest x1 4.05 us: dots_of(): pl.pallas_call(dots_kernel, grid=(4,), in_specs=[block, block, pl.BlockSp...]
    concatenate x2 -> x0, other arithmetic: 2.05 us -> none  [the longest x1 1.29 us: body(): both = jnp.concatenate([dots, slot_weight], axis=1)]
  transfers between devices with their start and end apart: 5 -> 5, of which waited for: 3 -> 3; matrix products, arithmetic and copies ran while one was open for 4% -> 3% of each run, Pallas kernels for 6% -> 6%
where the time goes in v4:
time: 173 us; the launch traced here: 172 us
  blocking collectives  62.1 us (36%)
  waiting for transfers between devices  37.3 us (22%)
  starting transfers between devices  35.3 us (20%)
  Pallas kernels  14.7 us (8%)
  between operations  14.2 us (8%)
  local copies, waits for them, and re-layouts  4.1 us (2%)
  other arithmetic  3.8 us (2%)
    all_to_all x1, blocking collectives, body(): first = lax.all_to_all(first, 'z', split_axis=0, concat_axis=0, tiled=True)  36.8 us
    all_to_all x1, blocking collectives, body(): lax.all_to_all(second, 'z', split_axis=0, concat_axis=0, tiled=True)  25.3 us
    all_to_all x1, starting transfers between devices, body(): lax.all_to_all(send, ('node', 'x'), split_axis=0, concat_axis=0, tiled=True)  19.4 us
    all_to_all x1, waiting for transfers between devices, body(): lax.all_to_all(send, ('node', 'x'), split_axis=0, concat_axis=0, tiled=True)  17.4 us
    all_to_all x1, waiting for transfers between devices, body(): lax.all_to_all(value, ('node', 'x'), split_axis=0, concat_axis=0, tiled=T...  13.4 us
    all_to_all x1, starting transfers between devices, body(): lax.all_to_all(value, ('node', 'x'), split_axis=0, concat_axis=0, tiled=T...  12.5 us
    all_to_all x1, waiting for transfers between devices, body(): both = lax.all_to_all(both, 'z', split_axis=0, concat_axis=0, tiled=True)  6.38 us
    pallas_call x1, Pallas kernels, product(): pl.pallas_call(product_kernel, grid=(units // LANES // per_step,), in_spe...  5.33 us
  transfers between devices with their start and end apart: 5, of which 3 were waited for; matrix products, arithmetic and copies ran while one was open for 3% of the time, Pallas kernels for 6%

profile of v4, /device:TPU:1, one launch (start us, length us, event | category | flops | bytes accessed | tf_op | source)
XLA Modules:
  0.0 171.6 jit_solution(11976810989088322675)
XLA Ops:
  7.2 0.9 copy-done.1
  8.1 0.7 copy-done.2
  8.8 0.7 copy-done.3
  9.4 1.6 shard_map.77
  11.0 19.4 %all-to-all-start = ((bf16[128,16,128]{2,1,0:T(8,128)(2,1)}), bf16[128,16,128]{2,1,0:T(8,128)(2,1)S(1)}, u32[]{:S(2)}, u32[]{:S(2)}) async-start(bf16[128,16,128]{2,1,0:T(8,128)(2,1)} %bitcast), calls=%async_computation | async-start | bytes 1048576 | tf_op jit(solution)/shard_map/all_to_all | solution.py:250
  30.4 1.9 %fusion.5 = bf16[1024,128]{1,0:T(8,128)(2,1)} fusion(bf16[1,1024,128]{2,1,0:T(8,128)(2,1)} %up_ref.1, bf16[1,1024,128]{2,1,0:T(8,128)(2,1)} %gate_ref.1), kind=kLoop, calls=%fused_computation.9 | loop fusion | flops 1048576 | bytes 786432 | tf_op jit(solution)/shard_map/convert_element_type | solution.py:245
  32.4 17.4 %all-to-all-done = bf16[128,16,128]{2,1,0:T(8,128)(2,1)S(1)} async-done(((bf16[128,16,128]{2,1,0:T(8,128)(2,1)}), bf16[128,16,128]{2,1,0:T(8,128)(2,1)S(1)}, u32[]{:S(2)}, u32[]{:S(2)}) %all-to-all-start) | async-done | bytes 524320 | tf_op jit(solution)/shard_map/all_to_all | solution.py:250
  49.9 0.2 slice_convert_fusion
  50.4 0.2 fusion
  50.7 0.3 copy.25
  51.1 0.2 copy.26.rows_ref
  51.4 1.4 shard_map.78
  52.8 36.8 %all_to_all.25.first_ref = bf16[8,64,896]{2,1,0:T(8,128)(2,1)S(1)} all-to-all(bf16[8,64,896]{2,1,0:T(8,128)(2,1)S(1)} %get-tuple-element.8), channel_id=1, replica_groups=mesh['node'=16,'z'=8,'x'=8] {'z'}, dimensions={0} | all-to-all | bytes 1835008 | tf_op jit(solution)/shard_map/all_to_all | solution.py:267
  89.6 25.3 %all_to_all.26.second_ref = bf16[8,64,896]{2,1,0:T(8,128)(2,1)S(1)} all-to-all(bf16[8,64,896]{2,1,0:T(8,128)(2,1)S(1)} %get-tuple-element.9), channel_id=1, replica_groups=mesh['node'=16,'z'=8,'x'=8] {'z'}, dimensions={0} | all-to-all | bytes 1835008 | tf_op jit(solution)/shard_map/all_to_all | solution.py:268
  114.9 5.3 %shard_map.79 = bf16[8,8,2,64,128]{4,3,2,1,0:T(8,128)(2,1)} custom-call(bf16[8,64,896]{2,1,0:T(8,128)(2,1)S(1)} %all_to_all.25.first_ref, bf16[8,64,896]{2,1,0:T(8,128)(2,1)S(1)} %all_to_all.26.second_ref, bf16[1,1024,896]{2,1,0:T(8,128)(2,1)} %weight_ref.1), custom_call_target="tpu_custom_call" | custom-call | flops 1879048192 | bytes 6000000 | tf_op jit(solution)/shard_map/pallas_call | solution.py:156
  120.3 4.1 %shard_map.80 = f32[8,2,128]{2,1,0:T(2,128)} custom-call(bf16[8,1024,128]{2,1,0:T(8,128)(2,1)} %bitcast.25, bf16[8,1024,128]{2,1,0:T(8,128)(2,1)} %bitcast.29, f32[8,1,128]{2,1,0:T(1,128)} %copy-done), custom_call_target="tpu_custom_call" | custom-call | flops 2097152 | bytes 4000000 | tf_op jit(solution)/shard_map/pallas_call | solution.py:184
  124.4 3.3 %all-to-all-start.3 = ((f32[8,2,128]{2,1,0:T(2,128)}), f32[8,2,128]{2,1,0:T(2,128)S(1)}, u32[]{:S(2)}, u32[]{:S(2)}) async-start(f32[8,2,128]{2,1,0:T(2,128)} %shard_map.80), calls=%async_computation.4 | async-start | bytes 16384 | tf_op jit(solution)/shard_map/all_to_all | solution.py:276
  127.8 6.4 %all-to-all-done.3.weight_ref = f32[8,2,128]{2,1,0:T(2,128)S(1)} async-done(((f32[8,2,128]{2,1,0:T(2,128)}), f32[8,2,128]{2,1,0:T(2,128)S(1)}, u32[]{:S(2)}, u32[]{:S(2)}) %all-to-all-start.3) | async-done | bytes 8224 | tf_op jit(solution)/shard_map/all_to_all | solution.py:276
  134.2 0.6 select_reduce_fusion
  134.9 0.8 copy.30
  135.7 12.5 %all-to-all-start.4 = ((f32[128,2,8]{2,1,0:T(2,128)}), f32[128,2,8]{2,1,0:T(2,128)S(1)}, u32[]{:S(2)}, u32[]{:S(2)}) async-start(f32[128,2,8]{2,1,0:T(2,128)} %bitcast.15), calls=%async_computation.5 | async-start | bytes 262144 | tf_op jit(solution)/shard_map/all_to_all | solution.py:285
  148.3 13.4 %all-to-all-done.4 = f32[128,2,8]{2,1,0:T(2,128)S(1)} async-done(((f32[128,2,8]{2,1,0:T(2,128)}), f32[128,2,8]{2,1,0:T(2,128)S(1)}, u32[]{:S(2)}, u32[]{:S(2)}) %all-to-all-start.4) | async-done | bytes 8224 | tf_op jit(solution)/shard_map/all_to_all | solution.py:285
  161.8 0.7 multiply_reduce_fusion
  162.5 2.3 %shard_map.81 = bf16[1,2,1024,128]{3,2,1,0:T(8,128)(2,1)} custom-call(bf16[1024,128]{1,0:T(8,128)(2,1)} %reduce-scatter.2.cloned.1.call-done.u_ref, bf16[1,1024,128]{2,1,0:T(8,128)(2,1)} %gate_ref.1, bf16[1,1024,128]{2,1,0:T(8,128)(2,1)} %up_ref.1, f32[8,2,128]{2,1,0:T(2,128)} %copy-done.4), custom_call_target="tpu_custom_call" | custom-call | flops 3932160 | bytes 2000000 | tf_op jit(solution)/shard_map/pallas_call | solution.py:213
  (28 shorter events, 1.0 us)
Async XLA Ops:
  7.2 0.9 copy-start.1
  8.1 0.7 copy-start.2
  8.8 0.7 copy-start.3
  11.0 38.9 %all-to-all-start = ((bf16[128,16,128]{2,1,0:T(8,128)(2,1)}), bf16[128,16,128]{2,1,0:T(8,128)(2,1)S(1)}, u32[]{:S(2)}, u32[]{:S(2)}) async-start(bf16[128,16,128]{2,1,0:T(8,128)(2,1)} %bitcast), calls=%async_computation | async-start | bytes 1048576 | tf_op jit(solution)/shard_map/all_to_all | solution.py:250
  30.4 89.9 %all-gather.2.cloned.1.call-start = ((), (), s32[]{:S(2)}) async-start(), calls=%async_computation.7 | async-start | bytes 2359296 | tf_op jit(solution)/shard_map/all_gather | solution.py:246
  32.4 130.1 %reduce-scatter.2.cloned.1.call-start = ((), (), s32[]{:S(2)}) async-start(), calls=%async_computation.6 | async-start | bytes 2359296 | tf_op jit(solution)/shard_map/reduce_scatter | solution.py:271
  52.8 36.8 %copy-start = (f32[8,1,128]{2,1,0:T(1,128)}, f32[8,1,128]{2,1,0:T(1,128)S(1)}, u32[]{:S(2)}) copy-start(f32[8,1,128]{2,1,0:T(1,128)S(1)} %get-tuple-element.10.weight_ref) | copy-start | bytes 12292
  124.4 9.9 %all-to-all-start.3 = ((f32[8,2,128]{2,1,0:T(2,128)}), f32[8,2,128]{2,1,0:T(2,128)S(1)}, u32[]{:S(2)}, u32[]{:S(2)}) async-start(f32[8,2,128]{2,1,0:T(2,128)} %shard_map.80), calls=%async_computation.4 | async-start | bytes 16384 | tf_op jit(solution)/shard_map/all_to_all | solution.py:276
  134.2 28.3 %copy-start.4 = (f32[8,2,128]{2,1,0:T(2,128)}, f32[8,2,128]{2,1,0:T(2,128)S(1)}, u32[]{:S(2)}) copy-start(f32[8,2,128]{2,1,0:T(2,128)S(1)} %all-to-all-done.3.weight_ref) | copy-start | bytes 24580
  135.7 25.9 %all-to-all-start.4 = ((f32[128,2,8]{2,1,0:T(2,128)}), f32[128,2,8]{2,1,0:T(2,128)S(1)}, u32[]{:S(2)}, u32[]{:S(2)}) async-start(f32[128,2,8]{2,1,0:T(2,128)} %bitcast.15), calls=%async_computation.5 | async-start | bytes 262144 | tf_op jit(solution)/shard_map/all_to_all | solution.py:285
Sparse Core Ops, SparseCore 0:
  33.9 48.9 all-gather.1
  120.4 39.3 reduce-scatter.1

commit v5 on v4

--- a/solution.py
+++ b/solution.py
@@ -73,24 +73,18 @@
             jax.ShapeDtypeStruct((nodes, slices, lines, LANES), BF16),
             jax.ShapeDtypeStruct((nodes * per_group, out_grad.shape[0]), F32),
         ],
-        compiler_params=pltpu.CompilerParams(vmem_limit_bytes=32 * 1024 * 1024),
+        compiler_params=pltpu.CompilerParams(vmem_limit_bytes=60 * 1024 * 1024),
         cost_estimate=pl.CostEstimate(flops=40_000_000, bytes_accessed=700_000, transcendentals=0),
     )(out_grad, expert_ids, route_weights)
 
 
-def pick_kernel(lines_ref, rows_ref, first_ref, second_ref, slot_weight_ref):
-    experts, half, _ = first_ref.shape
-    slots = 2 * half
+def pick_kernel(lines_ref, rows_ref, out_ref, slot_weight_ref):
+    experts, slots, _ = out_ref.shape
     row_count = rows_ref.shape[0]
     slot = lax.broadcasted_iota(jnp.int32, (slots, row_count), 0).astype(F32)
     for expert in range(experts):
         holds = jnp.where(lines_ref[expert : expert + 1, :] == slot, 1.0, 0.0).astype(BF16)
-        first_ref[expert] = jnp.dot(
-            holds[:half], rows_ref[...], preferred_element_type=F32
-        ).astype(BF16)
-        second_ref[expert] = jnp.dot(
-            holds[half:], rows_ref[...], preferred_element_type=F32
-        ).astype(BF16)
+        out_ref[expert] = jnp.dot(holds, rows_ref[...], preferred_element_type=F32).astype(BF16)
         weights = lines_ref[experts + expert : experts + expert + 1, :].astype(BF16)
         slot_weight_ref[expert] = lax.dot_general(
             jnp.broadcast_to(weights, (8, row_count)),
@@ -107,10 +101,9 @@
     return pl.pallas_call(
         pick_kernel,
         in_specs=[vmem, vmem],
-        out_specs=[vmem, vmem, vmem],
+        out_specs=[vmem, vmem],
         out_shape=[
-            jax.ShapeDtypeStruct((experts, slots // 2, width), BF16),
-            jax.ShapeDtypeStruct((experts, slots // 2, width), BF16),
+            jax.ShapeDtypeStruct((experts, slots, width), BF16),
             jax.ShapeDtypeStruct((experts, 1, slots), F32),
         ],
         compiler_params=pltpu.CompilerParams(vmem_limit_bytes=32 * 1024 * 1024),
@@ -136,34 +129,35 @@
     return jnp.sum(jnp.where(same, line, 0.0), axis=1, keepdims=True)
 
 
-def product_kernel(first_ref, second_ref, weight_ref, out_ref):
-    z_count, half, width = first_ref.shape
-    for part, rows_ref in enumerate((first_ref, second_ref)):
-        rows = rows_ref[...].reshape(z_count * half, width)
-        term = lax.dot_general(
-            rows, weight_ref[0], (((1,), (1,)), ((), ())), preferred_element_type=F32
-        ).astype(BF16)
-        for block in range(out_ref.shape[0]):
-            lanes = term[:, block * LANES : (block + 1) * LANES]
-            out_ref[block, :, part] = lanes.reshape(z_count, half, LANES)
-
-
-def product(first, second, weight):
-    z_count, half, width = first.shape
+def product_kernel(rows_ref, weight_ref, out_ref):
+    z_count, slots, width = rows_ref.shape
+    rows = rows_ref[...].reshape(z_count * slots, width)
+    term = lax.dot_general(
+        rows, weight_ref[0], (((1,), (1,)), ((), ())), preferred_element_type=F32
+    ).astype(BF16)
+    for block in range(out_ref.shape[0]):
+        out_ref[block] = term[:, block * LANES : (block + 1) * LANES]
+
+
+def product(rows, weight):
+    z_count, slots, width = rows.shape
     units = weight.shape[1]
-    per_step = 2
-    rows = pl.BlockSpec((z_count, half, width), lambda i: (0, 0, 0))
+    slot_count = z_count * slots
+    per_step = 4
     return pl.pallas_call(
         product_kernel,
         grid=(units // LANES // per_step,),
-        in_specs=[rows, rows, pl.BlockSpec((1, per_step * LANES, width), lambda i: (0, i, 0))],
-        out_specs=pl.BlockSpec((per_step, z_count, 2, half, LANES), lambda i: (i, 0, 0, 0, 0)),
-        out_shape=jax.ShapeDtypeStruct((units // LANES, z_count, 2, half, LANES), BF16),
+        in_specs=[
+            pl.BlockSpec((z_count, slots, width), lambda i: (0, 0, 0)),
+            pl.BlockSpec((1, per_step * LANES, width), lambda i: (0, i, 0)),
+        ],
+        out_specs=pl.BlockSpec((per_step, slot_count, LANES), lambda i: (i, 0, 0)),
+        out_shape=jax.ShapeDtypeStruct((units // LANES, slot_count, LANES), BF16),
         compiler_params=pltpu.CompilerParams(vmem_limit_bytes=52 * 1024 * 1024),
         cost_estimate=pl.CostEstimate(
-            flops=4 * z_count * half * width * units, bytes_accessed=6_000_000, transcendentals=0
-        ),
-    )(first, second, weight)
+            flops=2 * slot_count * width * units, bytes_accessed=6_000_000, transcendentals=0
+        ),
+    )(rows, weight)
 
 
 def dots_kernel(term_ref, hidden_ref, weight_ref, both_ref):
@@ -187,7 +181,7 @@
         in_specs=[block, block, pl.BlockSpec((per_step, 1, slots), lambda i: (i, 0, 0))],
         out_specs=pl.BlockSpec((per_step, 2, slots), lambda i: (i, 0, 0)),
         out_shape=jax.ShapeDtypeStruct((z_count, 2, slots), F32),
-        compiler_params=pltpu.CompilerParams(vmem_limit_bytes=60 * 1024 * 1024),
+        compiler_params=pltpu.CompilerParams(vmem_limit_bytes=62_390_272),
         cost_estimate=pl.CostEstimate(
             flops=2 * blocks * slot_count * lanes, bytes_accessed=4_000_000, transcendentals=0
         ),
@@ -221,7 +215,7 @@
         ],
         out_specs=pl.BlockSpec((1, 2, lines, width), lambda z: (0, 0, z, 0)),
         out_shape=jax.ShapeDtypeStruct((1, 2, slot_count, width), BF16),
-        compiler_params=pltpu.CompilerParams(vmem_limit_bytes=60 * 1024 * 1024),
+        compiler_params=pltpu.CompilerParams(vmem_limit_bytes=62_390_272),
         cost_estimate=pl.CostEstimate(
             flops=30 * slot_count * width, bytes_accessed=2_000_000, transcendentals=slot_count * width
         ),
@@ -263,11 +257,10 @@
     place = jnp.dot(earlier.astype(BF16), named_by.astype(BF16), preferred_element_type=F32)
     slot_each = jnp.where(named_by, (relay * cap_expert).astype(F32)[:, None] + place, -1.0)
     lines = jnp.concatenate([slot_each.T, weight_each.T], axis=0)
-    first, second, slot_weight = pick(lines, rows, slots)
-    first = lax.all_to_all(first, "z", split_axis=0, concat_axis=0, tiled=True)
-    second = lax.all_to_all(second, "z", split_axis=0, concat_axis=0, tiled=True)
-
-    partial = product(first, second, down_weight).reshape(n_x, n_z * slots, LANES)
+    picked, slot_weight = pick(lines, rows, slots)
+    taken = lax.all_to_all(picked, "z", split_axis=0, concat_axis=0, tiled=True)
+
+    partial = product(taken, down_weight)
     u = lax.psum_scatter(
         partial.reshape(n_x * n_z * slots, LANES), "x", scatter_dimension=0, tiled=True
     )

time: 173 us -> 162 us (0.936)
  blocking collectives: 62.1 us -> 56 us
  starting transfers between devices: 35.3 us -> 32.7 us
    all_to_all x2 -> x1, blocking collectives: 62.1 us -> 56 us  [body(): taken = lax.all_to_all(picked, 'z', split_axis=0, concat_axis=0, tiled=True)]
    all_to_all x1, starting transfers between devices: 12.5 us -> 9.91 us  [body(): lax.all_to_all(value, ('node', 'x'), split_axis=0, concat_axis=0, tiled=T...]
  transfers between devices with their start and end apart: 5 -> 5, of which waited for: 3 -> 3; matrix products, arithmetic and copies ran while one was open for 3% -> 4% of each run, Pallas kernels for 6% -> 6%
where the time goes in v5:
time: 162 us; the launch traced here: 161 us
  blocking collectives  56 us (35%)
  waiting for transfers between devices  37.6 us (23%)
  starting transfers between devices  32.7 us (20%)
  Pallas kernels  14.5 us (9%)
  between operations  14.2 us (9%)
  other arithmetic  3.8 us (2%)
  local copies, waits for them, and re-layouts  2.43 us (2%)
    all_to_all x1, blocking collectives, body(): taken = lax.all_to_all(picked, 'z', split_axis=0, concat_axis=0, tiled=True)  56 us
    all_to_all x1, starting transfers between devices, body(): lax.all_to_all(send, ('node', 'x'), split_axis=0, concat_axis=0, tiled=True)  19.4 us
    all_to_all x1, waiting for transfers between devices, body(): lax.all_to_all(send, ('node', 'x'), split_axis=0, concat_axis=0, tiled=True)  17.4 us
    all_to_all x1, waiting for transfers between devices, body(): lax.all_to_all(value, ('node', 'x'), split_axis=0, concat_axis=0, tiled=T...  13.7 us
    all_to_all x1, starting transfers between devices, body(): lax.all_to_all(value, ('node', 'x'), split_axis=0, concat_axis=0, tiled=T...  9.91 us
    all_to_all x1, waiting for transfers between devices, body(): both = lax.all_to_all(both, 'z', split_axis=0, concat_axis=0, tiled=True)  6.38 us
    pallas_call x1, Pallas kernels, product(): pl.pallas_call(product_kernel, grid=(units // LANES // per_step,), in_spe...  4.79 us
    pallas_call x1, Pallas kernels, dots_of(): pl.pallas_call(dots_kernel, grid=(4,), in_specs=[block, block, pl.BlockSp...  4.05 us
  transfers between devices with their start and end apart: 5, of which 3 were waited for; matrix products, arithmetic and copies ran while one was open for 4% of the time, Pallas kernels for 6%

profile of v5, /device:TPU:1, one launch (start us, length us, event | category | flops | bytes accessed | tf_op | source)
XLA Modules:
  0.0 161.5 jit_solution(9048016108958882642)
XLA Ops:
  7.2 2.5 %shard_map.77 = (bf16[16,8,16,128]{3,2,1,0:T(8,128)(2,1)}, f32[32,8]{1,0:T(8,128)}) custom-call(bf16[8,7168]{1,0:T(8,128)(2,1)} %grad_ref.1, s32[8,8]{1,0:T(8,128)} %ids_ref.1, bf16[8,8]{1,0:T(8,128)(2,1)} %weights_ref.1), custom_call_target="tpu_custom_call" | custom-call | flops 40000000 | bytes 700000 | tf_op jit(solution)/shard_map/pallas_call | solution.py:70
  9.7 19.4 %all-to-all-start = ((bf16[128,16,128]{2,1,0:T(8,128)(2,1)}), bf16[128,16,128]{2,1,0:T(8,128)(2,1)S(1)}, u32[]{:S(2)}, u32[]{:S(2)}) async-start(bf16[128,16,128]{2,1,0:T(8,128)(2,1)} %bitcast.28), calls=%async_computation | async-start | bytes 1048576 | tf_op jit(solution)/shard_map/all_to_all | solution.py:244
  29.1 1.9 %fusion.5 = bf16[1024,128]{1,0:T(8,128)(2,1)} fusion(bf16[1,1024,128]{2,1,0:T(8,128)(2,1)} %up_ref.1, bf16[1,1024,128]{2,1,0:T(8,128)(2,1)} %gate_ref.1), kind=kLoop, calls=%fused_computation.9 | loop fusion | flops 1048576 | bytes 786432 | tf_op jit(solution)/shard_map/convert_element_type | solution.py:239
  31.1 17.4 %all-to-all-done = bf16[128,16,128]{2,1,0:T(8,128)(2,1)S(1)} async-done(((bf16[128,16,128]{2,1,0:T(8,128)(2,1)}), bf16[128,16,128]{2,1,0:T(8,128)(2,1)S(1)}, u32[]{:S(2)}, u32[]{:S(2)}) %all-to-all-start) | async-done | bytes 524320 | tf_op jit(solution)/shard_map/all_to_all | solution.py:244
  48.5 0.2 slice_convert_fusion
  48.8 0.2 fusion.10
  49.1 0.2 fusion
  49.3 0.1 copy.24
  49.4 0.3 copy.25
  49.7 0.2 copy.26.rows_ref
  50.0 0.9 shard_map.78
  50.9 0.6 copy-done
  51.5 56.0 %all_to_all.20.rows_ref = bf16[8,128,896]{2,1,0:T(8,128)(2,1)S(1)} all-to-all(bf16[8,128,896]{2,1,0:T(8,128)(2,1)S(1)} %get-tuple-element.7), channel_id=1, replica_groups=mesh['node'=16,'z'=8,'x'=8] {'z'}, dimensions={0} | all-to-all | bytes 3670016 | tf_op jit(solution)/shard_map/all_to_all | solution.py:261
  107.5 4.8 %shard_map.79.term_ref = bf16[8,1024,128]{2,1,0:T(8,128)(2,1)} custom-call(bf16[8,128,896]{2,1,0:T(8,128)(2,1)S(1)} %all_to_all.20.rows_ref, bf16[1,1024,896]{2,1,0:T(8,128)(2,1)} %weight_ref.1), custom_call_target="tpu_custom_call" | custom-call | flops 1879048192 | bytes 6000000 | tf_op jit(solution)/shard_map/pallas_call | solution.py:147
  112.3 4.1 %shard_map.80 = f32[8,2,128]{2,1,0:T(2,128)} custom-call(bf16[8,1024,128]{2,1,0:T(8,128)(2,1)} %shard_map.79.term_ref, bf16[8,1024,128]{2,1,0:T(8,128)(2,1)} %bitcast.26, f32[8,1,128]{2,1,0:T(1,128)} %copy-done), custom_call_target="tpu_custom_call" | custom-call | flops 2097152 | bytes 4000000 | tf_op jit(solution)/shard_map/pallas_call | solution.py:178
  116.4 3.3 %all-to-all-start.2 = ((f32[8,2,128]{2,1,0:T(2,128)}), f32[8,2,128]{2,1,0:T(2,128)S(1)}, u32[]{:S(2)}, u32[]{:S(2)}) async-start(f32[8,2,128]{2,1,0:T(2,128)} %shard_map.80), calls=%async_computation.3 | async-start | bytes 16384 | tf_op jit(solution)/shard_map/all_to_all | solution.py:269
  119.7 0.1 copy.28
  119.9 6.4 %all-to-all-done.2.weight_ref = f32[8,2,128]{2,1,0:T(2,128)S(1)} async-done(((f32[8,2,128]{2,1,0:T(2,128)}), f32[8,2,128]{2,1,0:T(2,128)S(1)}, u32[]{:S(2)}, u32[]{:S(2)}) %all-to-all-start.2) | async-done | bytes 8224 | tf_op jit(solution)/shard_map/all_to_all | solution.py:269
  126.2 0.6 select_reduce_fusion
  127.0 0.8 copy.30
  127.8 9.9 %all-to-all-start.3 = ((f32[128,2,8]{2,1,0:T(2,128)}), f32[128,2,8]{2,1,0:T(2,128)S(1)}, u32[]{:S(2)}, u32[]{:S(2)}) async-start(f32[128,2,8]{2,1,0:T(2,128)} %bitcast.14), calls=%async_computation.4 | async-start | bytes 262144 | tf_op jit(solution)/shard_map/all_to_all | solution.py:278
  137.8 13.7 %all-to-all-done.3 = f32[128,2,8]{2,1,0:T(2,128)S(1)} async-done(((f32[128,2,8]{2,1,0:T(2,128)}), f32[128,2,8]{2,1,0:T(2,128)S(1)}, u32[]{:S(2)}, u32[]{:S(2)}) %all-to-all-start.3) | async-done | bytes 8224 | tf_op jit(solution)/shard_map/all_to_all | solution.py:278
  151.6 0.7 multiply_reduce_fusion
  152.3 2.3 %shard_map.81 = bf16[1,2,1024,128]{3,2,1,0:T(8,128)(2,1)} custom-call(bf16[1024,128]{1,0:T(8,128)(2,1)} %reduce-scatter.2.cloned.1.call-done.u_ref, bf16[1,1024,128]{2,1,0:T(8,128)(2,1)} %gate_ref.1, bf16[1,1024,128]{2,1,0:T(8,128)(2,1)} %up_ref.1, f32[8,2,128]{2,1,0:T(2,128)} %copy-done.1), custom_call_target="tpu_custom_call" | custom-call | flops 3932160 | bytes 2000000 | tf_op jit(solution)/shard_map/pallas_call | solution.py:207
  (23 shorter events, 0.6 us)
Async XLA Ops:
  9.7 38.9 %all-to-all-start = ((bf16[128,16,128]{2,1,0:T(8,128)(2,1)}), bf16[128,16,128]{2,1,0:T(8,128)(2,1)S(1)}, u32[]{:S(2)}, u32[]{:S(2)}) async-start(bf16[128,16,128]{2,1,0:T(8,128)(2,1)} %bitcast.28), calls=%async_computation | async-start | bytes 1048576 | tf_op jit(solution)/shard_map/all_to_all | solution.py:244
  29.0 83.3 %all-gather.2.cloned.1.call-start = ((), (), s32[]{:S(2)}) async-start(), calls=%async_computation.6 | async-start | bytes 2359296 | tf_op jit(solution)/shard_map/all_gather | solution.py:240
  31.0 121.3 %reduce-scatter.2.cloned.1.call-start = ((), (), s32[]{:S(2)}) async-start(), calls=%async_computation.5 | async-start | bytes 2359296 | tf_op jit(solution)/shard_map/reduce_scatter | solution.py:264
  50.9 0.6 copy-start
  112.3 25.4 %copy-start.2 = (f32[32,8]{1,0:T(8,128)S(1)}, f32[32,8]{1,0:T(8,128)}, u32[]{:S(2)}) copy-start(f32[32,8]{1,0:T(8,128)} %get-tuple-element.9) | copy-start | bytes 3076
  116.4 9.9 %all-to-all-start.2 = ((f32[8,2,128]{2,1,0:T(2,128)}), f32[8,2,128]{2,1,0:T(2,128)S(1)}, u32[]{:S(2)}, u32[]{:S(2)}) async-start(f32[8,2,128]{2,1,0:T(2,128)} %shard_map.80), calls=%async_computation.3 | async-start | bytes 16384 | tf_op jit(solution)/shard_map/all_to_all | solution.py:269
  126.2 26.1 %copy-start.1 = (f32[8,2,128]{2,1,0:T(2,128)}, f32[8,2,128]{2,1,0:T(2,128)S(1)}, u32[]{:S(2)}) copy-start(f32[8,2,128]{2,1,0:T(2,128)S(1)} %all-to-all-done.2.weight_ref) | copy-start | bytes 24580
  127.8 23.7 %all-to-all-start.3 = ((f32[128,2,8]{2,1,0:T(2,128)}), f32[128,2,8]{2,1,0:T(2,128)S(1)}, u32[]{:S(2)}, u32[]{:S(2)}) async-start(f32[128,2,8]{2,1,0:T(2,128)} %bitcast.14), calls=%async_computation.4 | async-start | bytes 262144 | tf_op jit(solution)/shard_map/all_to_all | solution.py:278
Sparse Core Ops, SparseCore 0:
  32.5 48.9 all-gather.1
  112.4 36.7 reduce-scatter.1

commit v6 on v5

--- a/solution.py
+++ b/solution.py
@@ -78,39 +78,66 @@
     )(out_grad, expert_ids, route_weights)
 
 
-def pick_kernel(lines_ref, rows_ref, out_ref, slot_weight_ref):
+def pick_kernel(
+    group_ref, tail_ref, rows_ref, out_ref, slot_weight_ref, named_ref, slot_ref, *, relays, per_group, cap_expert
+):
     experts, slots, _ = out_ref.shape
     row_count = rows_ref.shape[0]
-    slot = lax.broadcasted_iota(jnp.int32, (slots, row_count), 0).astype(F32)
+    top_count = named_ref.shape[0] // 2
+    lines = (2 * top_count, LANES)
+    named = lax.dot_general(
+        one_where(iota(lines, 0) == iota(lines, 1)).astype(BF16),
+        tail_ref[...],
+        (((1,), (1,)), ((), ())),
+        preferred_element_type=F32,
+    )
+    named_ref[...] = named
+    own = named[:top_count] - (group_ref[0] * experts).astype(F32)
+    takes, weights = [], []
     for expert in range(experts):
-        holds = jnp.where(lines_ref[expert : expert + 1, :] == slot, 1.0, 0.0).astype(BF16)
+        hits = one_where(own == float(expert))
+        takes.append(jnp.sum(hits, axis=0, keepdims=True))
+        weights.append(jnp.sum(hits * named[top_count:], axis=0, keepdims=True))
+    takes = jnp.concatenate(takes, axis=0)
+    square = (row_count, row_count)
+    above, here = iota(square, 0), iota(square, 1)
+    same_relay = above // per_group % relays == here // per_group % relays
+    earlier = one_where((above < here) & same_relay).astype(BF16)
+    place = jnp.dot(takes.astype(BF16), earlier, preferred_element_type=F32)
+    relay = iota((experts, row_count), 1) // per_group % relays
+    slot_each = jnp.where(takes > 0.0, (relay * cap_expert).astype(F32) + place, -1.0)
+    slot_ref[...] = slot_each
+    slot = iota((slots, row_count), 0).astype(F32)
+    for expert in range(experts):
+        holds = one_where(slot_each[expert : expert + 1, :] == slot).astype(BF16)
         out_ref[expert] = jnp.dot(holds, rows_ref[...], preferred_element_type=F32).astype(BF16)
-        weights = lines_ref[experts + expert : experts + expert + 1, :].astype(BF16)
         slot_weight_ref[expert] = lax.dot_general(
-            jnp.broadcast_to(weights, (8, row_count)),
+            jnp.broadcast_to(weights[expert], (8, row_count)).astype(BF16),
             holds,
             (((1,), (1,)), ((), ())),
             preferred_element_type=F32,
         )[:1]
 
 
-def pick(lines, rows, slots):
-    experts = lines.shape[0] // 2
+def pick(group, tail, rows, experts, top_count, relays, per_group, cap_expert):
     row_count, width = rows.shape
+    slots = relays * cap_expert
     vmem = pl.BlockSpec(memory_space=pltpu.VMEM)
     return pl.pallas_call(
-        pick_kernel,
-        in_specs=[vmem, vmem],
-        out_specs=[vmem, vmem],
+        functools.partial(pick_kernel, relays=relays, per_group=per_group, cap_expert=cap_expert),
+        in_specs=[pl.BlockSpec(memory_space=pltpu.SMEM), vmem, vmem],
+        out_specs=[vmem] * 4,
         out_shape=[
             jax.ShapeDtypeStruct((experts, slots, width), BF16),
             jax.ShapeDtypeStruct((experts, 1, slots), F32),
+            jax.ShapeDtypeStruct((2 * top_count, row_count), F32),
+            jax.ShapeDtypeStruct((experts, row_count), F32),
         ],
         compiler_params=pltpu.CompilerParams(vmem_limit_bytes=32 * 1024 * 1024),
         cost_estimate=pl.CostEstimate(
             flops=2 * experts * slots * row_count * width, bytes_accessed=2_500_000, transcendentals=0
         ),
-    )(lines, rows)
+    )(group, tail, rows)
 
 
 def as_line(column):
@@ -181,7 +208,7 @@
         in_specs=[block, block, pl.BlockSpec((per_step, 1, slots), lambda i: (i, 0, 0))],
         out_specs=pl.BlockSpec((per_step, 2, slots), lambda i: (i, 0, 0)),
         out_shape=jax.ShapeDtypeStruct((z_count, 2, slots), F32),
-        compiler_params=pltpu.CompilerParams(vmem_limit_bytes=62_390_272),
+        compiler_params=pltpu.CompilerParams(vmem_limit_bytes=52 * 1024 * 1024),
         cost_estimate=pl.CostEstimate(
             flops=2 * blocks * slot_count * lanes, bytes_accessed=4_000_000, transcendentals=0
         ),
@@ -215,7 +242,7 @@
         ],
         out_specs=pl.BlockSpec((1, 2, lines, width), lambda z: (0, 0, z, 0)),
         out_shape=jax.ShapeDtypeStruct((1, 2, slot_count, width), BF16),
-        compiler_params=pltpu.CompilerParams(vmem_limit_bytes=62_390_272),
+        compiler_params=pltpu.CompilerParams(vmem_limit_bytes=60 * 1024 * 1024),
         cost_estimate=pl.CostEstimate(
             flops=30 * slot_count * width, bytes_accessed=2_000_000, transcendentals=slot_count * width
         ),
@@ -245,19 +272,10 @@
     got = got.reshape(row_count, tiles + 1, LANES)
 
     rows = got[:, :tiles].reshape(row_count, width)
-    ids = got[:, tiles, :top_count].astype(F32).astype(jnp.int32)
-    weights = got[:, tiles, top_count : 2 * top_count].astype(F32)
-    my_group = lax.axis_index("node")
-    member = (ids - my_group * n_z)[:, None, :] == jnp.arange(n_z, dtype=jnp.int32)[None, :, None]
-    named_by = jnp.any(member, axis=2)
-    weight_each = jnp.sum(jnp.where(member, weights[:, None, :], 0.0), axis=2)
-    row = jnp.arange(row_count, dtype=jnp.int32)
-    relay = row // cap_group % n_x
-    earlier = (row[None, :] < row[:, None]) & (relay[None, :] == relay[:, None])
-    place = jnp.dot(earlier.astype(BF16), named_by.astype(BF16), preferred_element_type=F32)
-    slot_each = jnp.where(named_by, (relay * cap_expert).astype(F32)[:, None] + place, -1.0)
-    lines = jnp.concatenate([slot_each.T, weight_each.T], axis=0)
-    picked, slot_weight = pick(lines, rows, slots)
+    group = lax.axis_index("node").astype(jnp.int32).reshape(1)
+    picked, slot_weight, named, slot_each = pick(
+        group, got[:, tiles], rows, n_z, top_count, n_x, cap_group, cap_expert
+    )
     taken = lax.all_to_all(picked, "z", split_axis=0, concat_axis=0, tiled=True)
 
     partial = product(taken, down_weight)
@@ -271,8 +289,10 @@
     grad_pre = gate(u, gate_pre, up_pre, both)
     slot_iota = jnp.arange(slots, dtype=jnp.int32).astype(F32)
     value = jnp.sum(
-        jnp.where(slot_each[:, :, None] == slot_iota, dots[None], 0.0), axis=2
-    )
+        jnp.where(slot_each.T[:, :, None] == slot_iota, dots[None], 0.0), axis=2
+    )
+    own = named[:top_count].T - (group[0] * n_z).astype(F32)
+    member = own[:, None, :] == jnp.arange(n_z, dtype=jnp.int32).astype(F32)[None, :, None]
     value = jnp.sum(jnp.where(member, value[:, :, None], 0.0), axis=1)
     value = value.reshape(n_node * n_x, cap_group, top_count)
     back = lax.all_to_all(value, ("node", "x"), split_axis=0, concat_axis=0, tiled=True)

time: 162 us -> 161 us (level)
  transfers between devices with their start and end apart: 5 -> 5, of which waited for: 3 -> 3; matrix products, arithmetic and copies ran while one was open for 4% -> 3% of each run, Pallas kernels for 6% -> 6%
where the time goes in v6:
time: 161 us
  blocking collectives  56 us (35%)
  waiting for transfers between devices  37.7 us (23%)
  starting transfers between devices  32.7 us (20%)
  Pallas kernels  14.8 us (9%)
  between operations  14.2 us (9%)
  other arithmetic  3.35 us (2%)
  local copies, waits for them, and re-layouts  1.85 us (1%)
    all_to_all x1, blocking collectives, body(): taken = lax.all_to_all(picked, 'z', split_axis=0, concat_axis=0, tiled=True)  56 us
    all_to_all x1, starting transfers between devices, body(): lax.all_to_all(send, ('node', 'x'), split_axis=0, concat_axis=0, tiled=True)  19.4 us
    all_to_all x1, waiting for transfers between devices, body(): lax.all_to_all(send, ('node', 'x'), split_axis=0, concat_axis=0, tiled=True)  17.4 us
    all_to_all x1, waiting for transfers between devices, body(): lax.all_to_all(value, ('node', 'x'), split_axis=0, concat_axis=0, tiled=T...  13.9 us
    all_to_all x1, starting transfers between devices, body(): lax.all_to_all(value, ('node', 'x'), split_axis=0, concat_axis=0, tiled=T...  9.91 us
    all_to_all x1, waiting for transfers between devices, body(): both = lax.all_to_all(both, 'z', split_axis=0, concat_axis=0, tiled=True)  6.37 us
    pallas_call x1, Pallas kernels, product(): pl.pallas_call(product_kernel, grid=(units // LANES // per_step,), in_spe...  4.78 us
    pallas_call x1, Pallas kernels, dots_of(): pl.pallas_call(dots_kernel, grid=(4,), in_specs=[block, block, pl.BlockSp...  4.05 us
  transfers between devices with their start and end apart: 5, of which 3 were waited for; matrix products, arithmetic and copies ran while one was open for 3% of the time, Pallas kernels for 6%

profile of v6, /device:TPU:1, one launch (start us, length us, event | category | flops | bytes accessed | tf_op | source)
XLA Modules:
  0.0 160.6 jit_solution(3550567568787037622)
XLA Ops:
  7.2 2.5 %shard_map.77 = (bf16[16,8,16,128]{3,2,1,0:T(8,128)(2,1)}, f32[32,8]{1,0:T(8,128)}) custom-call(bf16[8,7168]{1,0:T(8,128)(2,1)} %grad_ref.1, s32[8,8]{1,0:T(8,128)} %ids_ref.1, bf16[8,8]{1,0:T(8,128)(2,1)} %weights_ref.1), custom_call_target="tpu_custom_call" | custom-call | flops 40000000 | bytes 700000 | tf_op jit(solution)/shard_map/pallas_call | solution.py:70
  9.7 19.4 %all-to-all-start = ((bf16[128,16,128]{2,1,0:T(8,128)(2,1)}), bf16[128,16,128]{2,1,0:T(8,128)(2,1)S(1)}, u32[]{:S(2)}, u32[]{:S(2)}) async-start(bf16[128,16,128]{2,1,0:T(8,128)(2,1)} %bitcast.31), calls=%async_computation | async-start | bytes 1048576 | tf_op jit(solution)/shard_map/all_to_all | solution.py:271
  29.1 1.9 %fusion.4 = bf16[1024,128]{1,0:T(8,128)(2,1)} fusion(bf16[1,1024,128]{2,1,0:T(8,128)(2,1)} %up_ref.1, bf16[1,1024,128]{2,1,0:T(8,128)(2,1)} %gate_ref.1), kind=kLoop, calls=%fused_computation.7 | loop fusion | flops 1048576 | bytes 786432 | tf_op jit(solution)/shard_map/convert_element_type | solution.py:266
  31.1 17.4 %all-to-all-done = bf16[128,16,128]{2,1,0:T(8,128)(2,1)S(1)} async-done(((bf16[128,16,128]{2,1,0:T(8,128)(2,1)}), bf16[128,16,128]{2,1,0:T(8,128)(2,1)S(1)}, u32[]{:S(2)}, u32[]{:S(2)}) %all-to-all-start) | async-done | bytes 524320 | tf_op jit(solution)/shard_map/all_to_all | solution.py:271
  48.5 0.1 slice.16
  48.7 0.3 copy.23
  49.0 0.2 copy.24.rows_ref
  49.3 1.2 shard_map.78
  50.4 56.0 %all_to_all.20.rows_ref = bf16[8,128,896]{2,1,0:T(8,128)(2,1)S(1)} all-to-all(bf16[8,128,896]{2,1,0:T(8,128)(2,1)S(1)} %get-tuple-element.9), channel_id=1, replica_groups=mesh['node'=16,'z'=8,'x'=8] {'z'}, dimensions={0} | all-to-all | bytes 3670016 | tf_op jit(solution)/shard_map/all_to_all | solution.py:279
  106.4 4.8 %shard_map.79.term_ref = bf16[8,1024,128]{2,1,0:T(8,128)(2,1)} custom-call(bf16[8,128,896]{2,1,0:T(8,128)(2,1)S(1)} %all_to_all.20.rows_ref, bf16[1,1024,896]{2,1,0:T(8,128)(2,1)} %weight_ref.1), custom_call_target="tpu_custom_call" | custom-call | flops 1879048192 | bytes 6000000 | tf_op jit(solution)/shard_map/pallas_call | solution.py:174
  111.3 4.1 %shard_map.80 = f32[8,2,128]{2,1,0:T(2,128)} custom-call(bf16[8,1024,128]{2,1,0:T(8,128)(2,1)} %shard_map.79.term_ref, bf16[8,1024,128]{2,1,0:T(8,128)(2,1)} %bitcast.29, f32[8,1,128]{2,1,0:T(1,128)S(1)} %get-tuple-element.10.weight_ref), custom_call_target="tpu_custom_call" | custom-call | flops 2097152 | bytes 4000000 | tf_op jit(solution)/shard_map/pallas_call | solution.py:205
  115.3 3.3 %all-to-all-start.2 = ((f32[8,2,128]{2,1,0:T(2,128)}), f32[8,2,128]{2,1,0:T(2,128)S(1)}, u32[]{:S(2)}, u32[]{:S(2)}) async-start(f32[8,2,128]{2,1,0:T(2,128)} %shard_map.80), calls=%async_computation.3 | async-start | bytes 16384 | tf_op jit(solution)/shard_map/all_to_all | solution.py:287
  118.7 0.1 copy.26
  118.8 6.4 %all-to-all-done.2.weight_ref = f32[8,2,128]{2,1,0:T(2,128)S(1)} async-done(((f32[8,2,128]{2,1,0:T(2,128)}), f32[8,2,128]{2,1,0:T(2,128)S(1)}, u32[]{:S(2)}, u32[]{:S(2)}) %all-to-all-start.2) | async-done | bytes 8224 | tf_op jit(solution)/shard_map/all_to_all | solution.py:287
  125.2 0.6 select_reduce_fusion
  125.8 0.1 copy.27
  125.9 0.1 select_reduce_fusion.1
  126.0 0.8 copy.28
  126.8 9.9 %all-to-all-start.3 = ((f32[128,2,8]{2,1,0:T(2,128)}), f32[128,2,8]{2,1,0:T(2,128)S(1)}, u32[]{:S(2)}, u32[]{:S(2)}) async-start(f32[128,2,8]{2,1,0:T(2,128)} %bitcast.14), calls=%async_computation.4 | async-start | bytes 262144 | tf_op jit(solution)/shard_map/all_to_all | solution.py:298
  136.7 0.1 copy.25
  136.8 13.9 %all-to-all-done.3 = f32[128,2,8]{2,1,0:T(2,128)S(1)} async-done(((f32[128,2,8]{2,1,0:T(2,128)}), f32[128,2,8]{2,1,0:T(2,128)S(1)}, u32[]{:S(2)}, u32[]{:S(2)}) %all-to-all-start.3) | async-done | bytes 8224 | tf_op jit(solution)/shard_map/all_to_all | solution.py:298
  150.7 0.1 copy.33
  150.7 0.7 multiply_reduce_fusion
  151.4 2.3 %shard_map.81 = bf16[1,2,1024,128]{3,2,1,0:T(8,128)(2,1)} custom-call(bf16[1024,128]{1,0:T(8,128)(2,1)} %reduce-scatter.2.cloned.1.call-done.u_ref, bf16[1,1024,128]{2,1,0:T(8,128)(2,1)} %gate_ref.1, bf16[1,1024,128]{2,1,0:T(8,128)(2,1)} %up_ref.1, f32[8,2,128]{2,1,0:T(2,128)} %copy-done), custom_call_target="tpu_custom_call" | custom-call | flops 3932160 | bytes 2000000 | tf_op jit(solution)/shard_map/pallas_call | solution.py:234
  (16 shorter events, 0.2 us)
Async XLA Ops:
  9.7 38.9 %all-to-all-start = ((bf16[128,16,128]{2,1,0:T(8,128)(2,1)}), bf16[128,16,128]{2,1,0:T(8,128)(2,1)S(1)}, u32[]{:S(2)}, u32[]{:S(2)}) async-start(bf16[128,16,128]{2,1,0:T(8,128)(2,1)} %bitcast.31), calls=%async_computation | async-start | bytes 1048576 | tf_op jit(solution)/shard_map/all_to_all | solution.py:271
  29.0 82.2 %all-gather.2.cloned.1.call-start = ((), (), s32[]{:S(2)}) async-start(), calls=%async_computation.6 | async-start | bytes 2359296 | tf_op jit(solution)/shard_map/all_gather | solution.py:267
  31.0 120.4 %reduce-scatter.2.cloned.1.call-start = ((), (), s32[]{:S(2)}) async-start(), calls=%async_computation.5 | async-start | bytes 2359296 | tf_op jit(solution)/shard_map/reduce_scatter | solution.py:282
  111.2 25.4 %copy-start.1 = (f32[32,8]{1,0:T(8,128)S(1)}, f32[32,8]{1,0:T(8,128)}, u32[]{:S(2)}) copy-start(f32[32,8]{1,0:T(8,128)} %get-tuple-element.11) | copy-start | bytes 3076
  115.3 9.9 %all-to-all-start.2 = ((f32[8,2,128]{2,1,0:T(2,128)}), f32[8,2,128]{2,1,0:T(2,128)S(1)}, u32[]{:S(2)}, u32[]{:S(2)}) async-start(f32[8,2,128]{2,1,0:T(2,128)} %shard_map.80), calls=%async_computation.3 | async-start | bytes 16384 | tf_op jit(solution)/shard_map/all_to_all | solution.py:287
  125.2 26.3 %copy-start = (f32[8,2,128]{2,1,0:T(2,128)}, f32[8,2,128]{2,1,0:T(2,128)S(1)}, u32[]{:S(2)}) copy-start(f32[8,2,128]{2,1,0:T(2,128)S(1)} %all-to-all-done.2.weight_ref) | copy-start | bytes 24580
  126.8 23.9 %all-to-all-start.3 = ((f32[128,2,8]{2,1,0:T(2,128)}), f32[128,2,8]{2,1,0:T(2,128)S(1)}, u32[]{:S(2)}, u32[]{:S(2)}) async-start(f32[128,2,8]{2,1,0:T(2,128)} %bitcast.14), calls=%async_computation.4 | async-start | bytes 262144 | tf_op jit(solution)/shard_map/all_to_all | solution.py:298
Sparse Core Ops, SparseCore 0:
  32.5 48.9 all-gather.1
  111.3 36.8 reduce-scatter.1

commit v7 on v6

--- a/solution.py
+++ b/solution.py
@@ -229,11 +229,11 @@
 def gate(u, gate_pre, up_pre, both):
     z_count, _, slots = both.shape
     slot_count, width = u.shape
-    per_step = z_count // 2
+    per_step = z_count // 4
     lines = per_step * slots
     return pl.pallas_call(
         gate_kernel,
-        grid=(2,),
+        grid=(4,),
         in_specs=[
             pl.BlockSpec((lines, width), lambda z: (z, 0)),
             pl.BlockSpec((1, lines, width), lambda z: (0, z, 0)),

time: 161 us -> 162 us (level)
  no operation moved by 1% of the time
where the time goes in v7:
time: 162 us
  blocking collectives  56 us (35%)
  waiting for transfers between devices  37.7 us (23%)
  starting transfers between devices  32.7 us (20%)
  Pallas kernels  16.1 us (10%)
  between operations  14.2 us (9%)
  other arithmetic  3.35 us (2%)
  local copies, waits for them, and re-layouts  1.85 us (1%)
    all_to_all x1, blocking collectives, body(): taken = lax.all_to_all(picked, 'z', split_axis=0, concat_axis=0, tiled=True)  56 us
    all_to_all x1, starting transfers between devices, body(): lax.all_to_all(send, ('node', 'x'), split_axis=0, concat_axis=0, tiled=True)  19.4 us
    all_to_all x1, waiting for transfers between devices, body(): lax.all_to_all(send, ('node', 'x'), split_axis=0, concat_axis=0, tiled=True)  17.4 us
    all_to_all x1, waiting for transfers between devices, body(): lax.all_to_all(value, ('node', 'x'), split_axis=0, concat_axis=0, tiled=T...  13.9 us
    all_to_all x1, starting transfers between devices, body(): lax.all_to_all(value, ('node', 'x'), split_axis=0, concat_axis=0, tiled=T...  9.91 us
    all_to_all x1, waiting for transfers between devices, body(): both = lax.all_to_all(both, 'z', split_axis=0, concat_axis=0, tiled=True)  6.37 us
    pallas_call x1, Pallas kernels, product(): pl.pallas_call(product_kernel, grid=(units // LANES // per_step,), in_spe...  4.78 us
    pallas_call x1, Pallas kernels, dots_of(): pl.pallas_call(dots_kernel, grid=(4,), in_specs=[block, block, pl.BlockSp...  4.05 us
  transfers between devices with their start and end apart: 5, of which 3 were waited for; matrix products, arithmetic and copies ran while one was open for 3% of the time, Pallas kernels for 6%

profile of v7, /device:TPU:1, one launch (start us, length us, event | category | flops | bytes accessed | tf_op | source)
XLA Modules:
  0.0 161.8 jit_solution(6484773424289940510)
XLA Ops:
  7.2 2.5 %shard_map.77 = (bf16[16,8,16,128]{3,2,1,0:T(8,128)(2,1)}, f32[32,8]{1,0:T(8,128)}) custom-call(bf16[8,7168]{1,0:T(8,128)(2,1)} %grad_ref.1, s32[8,8]{1,0:T(8,128)} %ids_ref.1, bf16[8,8]{1,0:T(8,128)(2,1)} %weights_ref.1), custom_call_target="tpu_custom_call" | custom-call | flops 40000000 | bytes 700000 | tf_op jit(solution)/shard_map/pallas_call | solution.py:70
  9.7 19.4 %all-to-all-start = ((bf16[128,16,128]{2,1,0:T(8,128)(2,1)}), bf16[128,16,128]{2,1,0:T(8,128)(2,1)S(1)}, u32[]{:S(2)}, u32[]{:S(2)}) async-start(bf16[128,16,128]{2,1,0:T(8,128)(2,1)} %bitcast.31), calls=%async_computation | async-start | bytes 1048576 | tf_op jit(solution)/shard_map/all_to_all | solution.py:271
  29.1 1.9 %fusion.4 = bf16[1024,128]{1,0:T(8,128)(2,1)} fusion(bf16[1,1024,128]{2,1,0:T(8,128)(2,1)} %up_ref.1, bf16[1,1024,128]{2,1,0:T(8,128)(2,1)} %gate_ref.1), kind=kLoop, calls=%fused_computation.7 | loop fusion | flops 1048576 | bytes 786432 | tf_op jit(solution)/shard_map/convert_element_type | solution.py:266
  31.1 17.4 %all-to-all-done = bf16[128,16,128]{2,1,0:T(8,128)(2,1)S(1)} async-done(((bf16[128,16,128]{2,1,0:T(8,128)(2,1)}), bf16[128,16,128]{2,1,0:T(8,128)(2,1)S(1)}, u32[]{:S(2)}, u32[]{:S(2)}) %all-to-all-start) | async-done | bytes 524320 | tf_op jit(solution)/shard_map/all_to_all | solution.py:271
  48.5 0.1 slice.16
  48.7 0.3 copy.23
  49.0 0.2 copy.24.rows_ref
  49.3 1.2 shard_map.78
  50.4 56.0 %all_to_all.20.rows_ref = bf16[8,128,896]{2,1,0:T(8,128)(2,1)S(1)} all-to-all(bf16[8,128,896]{2,1,0:T(8,128)(2,1)S(1)} %get-tuple-element.9), channel_id=1, replica_groups=mesh['node'=16,'z'=8,'x'=8] {'z'}, dimensions={0} | all-to-all | bytes 3670016 | tf_op jit(solution)/shard_map/all_to_all | solution.py:279
  106.4 4.8 %shard_map.79.term_ref = bf16[8,1024,128]{2,1,0:T(8,128)(2,1)} custom-call(bf16[8,128,896]{2,1,0:T(8,128)(2,1)S(1)} %all_to_all.20.rows_ref, bf16[1,1024,896]{2,1,0:T(8,128)(2,1)} %weight_ref.1), custom_call_target="tpu_custom_call" | custom-call | flops 1879048192 | bytes 6000000 | tf_op jit(solution)/shard_map/pallas_call | solution.py:174
  111.3 4.1 %shard_map.80 = f32[8,2,128]{2,1,0:T(2,128)} custom-call(bf16[8,1024,128]{2,1,0:T(8,128)(2,1)} %shard_map.79.term_ref, bf16[8,1024,128]{2,1,0:T(8,128)(2,1)} %bitcast.29, f32[8,1,128]{2,1,0:T(1,128)S(1)} %get-tuple-element.10.weight_ref), custom_call_target="tpu_custom_call" | custom-call | flops 2097152 | bytes 4000000 | tf_op jit(solution)/shard_map/pallas_call | solution.py:205
  115.3 3.3 %all-to-all-start.2 = ((f32[8,2,128]{2,1,0:T(2,128)}), f32[8,2,128]{2,1,0:T(2,128)S(1)}, u32[]{:S(2)}, u32[]{:S(2)}) async-start(f32[8,2,128]{2,1,0:T(2,128)} %shard_map.80), calls=%async_computation.3 | async-start | bytes 16384 | tf_op jit(solution)/shard_map/all_to_all | solution.py:287
  118.7 0.1 copy.26
  118.8 6.4 %all-to-all-done.2.weight_ref = f32[8,2,128]{2,1,0:T(2,128)S(1)} async-done(((f32[8,2,128]{2,1,0:T(2,128)}), f32[8,2,128]{2,1,0:T(2,128)S(1)}, u32[]{:S(2)}, u32[]{:S(2)}) %all-to-all-start.2) | async-done | bytes 8224 | tf_op jit(solution)/shard_map/all_to_all | solution.py:287
  125.2 0.6 select_reduce_fusion
  125.8 0.1 copy.27
  125.9 0.1 select_reduce_fusion.1
  126.0 0.8 copy.28
  126.8 9.9 %all-to-all-start.3 = ((f32[128,2,8]{2,1,0:T(2,128)}), f32[128,2,8]{2,1,0:T(2,128)S(1)}, u32[]{:S(2)}, u32[]{:S(2)}) async-start(f32[128,2,8]{2,1,0:T(2,128)} %bitcast.14), calls=%async_computation.4 | async-start | bytes 262144 | tf_op jit(solution)/shard_map/all_to_all | solution.py:298
  136.7 0.1 copy.25
  136.8 13.9 %all-to-all-done.3 = f32[128,2,8]{2,1,0:T(2,128)S(1)} async-done(((f32[128,2,8]{2,1,0:T(2,128)}), f32[128,2,8]{2,1,0:T(2,128)S(1)}, u32[]{:S(2)}, u32[]{:S(2)}) %all-to-all-start.3) | async-done | bytes 8224 | tf_op jit(solution)/shard_map/all_to_all | solution.py:298
  150.7 0.1 copy.33
  150.7 0.7 multiply_reduce_fusion
  151.4 3.6 %shard_map.81 = bf16[1,2,1024,128]{3,2,1,0:T(8,128)(2,1)} custom-call(bf16[1024,128]{1,0:T(8,128)(2,1)} %reduce-scatter.2.cloned.1.call-done.u_ref, bf16[1,1024,128]{2,1,0:T(8,128)(2,1)} %gate_ref.1, bf16[1,1024,128]{2,1,0:T(8,128)(2,1)} %up_ref.1, f32[8,2,128]{2,1,0:T(2,128)} %copy-done), custom_call_target="tpu_custom_call" | custom-call | flops 3932160 | bytes 2000000 | tf_op jit(solution)/shard_map/pallas_call | solution.py:234
  (16 shorter events, 0.2 us)
Async XLA Ops:
  9.7 38.9 %all-to-all-start = ((bf16[128,16,128]{2,1,0:T(8,128)(2,1)}), bf16[128,16,128]{2,1,0:T(8,128)(2,1)S(1)}, u32[]{:S(2)}, u32[]{:S(2)}) async-start(bf16[128,16,128]{2,1,0:T(8,128)(2,1)} %bitcast.31), calls=%async_computation | async-start | bytes 1048576 | tf_op jit(solution)/shard_map/all_to_all | solution.py:271
  29.0 82.2 %all-gather.2.cloned.1.call-start = ((), (), s32[]{:S(2)}) async-start(), calls=%async_computation.6 | async-start | bytes 2359296 | tf_op jit(solution)/shard_map/all_gather | solution.py:267
  31.0 120.4 %reduce-scatter.2.cloned.1.call-start = ((), (), s32[]{:S(2)}) async-start(), calls=%async_computation.5 | async-start | bytes 2359296 | tf_op jit(solution)/shard_map/reduce_scatter | solution.py:282
  111.2 25.4 %copy-start.1 = (f32[32,8]{1,0:T(8,128)S(1)}, f32[32,8]{1,0:T(8,128)}, u32[]{:S(2)}) copy-start(f32[32,8]{1,0:T(8,128)} %get-tuple-element.11) | copy-start | bytes 3076
  115.3 9.9 %all-to-all-start.2 = ((f32[8,2,128]{2,1,0:T(2,128)}), f32[8,2,128]{2,1,0:T(2,128)S(1)}, u32[]{:S(2)}, u32[]{:S(2)}) async-start(f32[8,2,128]{2,1,0:T(2,128)} %shard_map.80), calls=%async_computation.3 | async-start | bytes 16384 | tf_op jit(solution)/shard_map/all_to_all | solution.py:287
  125.2 26.3 %copy-start = (f32[8,2,128]{2,1,0:T(2,128)}, f32[8,2,128]{2,1,0:T(2,128)S(1)}, u32[]{:S(2)}) copy-start(f32[8,2,128]{2,1,0:T(2,128)S(1)} %all-to-all-done.2.weight_ref) | copy-start | bytes 24580
  126.8 23.9 %all-to-all-start.3 = ((f32[128,2,8]{2,1,0:T(2,128)}), f32[128,2,8]{2,1,0:T(2,128)S(1)}, u32[]{:S(2)}, u32[]{:S(2)}) async-start(f32[128,2,8]{2,1,0:T(2,128)} %bitcast.14), calls=%async_computation.4 | async-start | bytes 262144 | tf_op jit(solution)/shard_map/all_to_all | solution.py:298
Sparse Core Ops, SparseCore 0:
  32.5 48.9 all-gather.1
  111.3 36.8 reduce-scatter.1
